TPU v7x, 32 devices: a whole 2x2x4 slice. The times are simulated.
32 devices in a mesh: section: 4 (over z), dp: 4 (over x, core), space: 2 (over y).
Axes of the slice: x: 2, y: 2, z: 4, core: 2. Of those that a mesh axis runs over, the one named last changes fastest.
Arguments:
- inputs: bfloat16 [4, 2, 4, 2, 8, 8, 256], P('section', None, 'dp', 'space'), may hold values from -6 to 6
- preacts: bfloat16 [4, 2, 4, 2, 8, 8, 256], P('section', None, 'dp', 'space'), may hold values from -6 to 6
- out_grad: bfloat16 [2, 4, 2, 8, 8, 256], P(None, 'dp', 'space'), may hold values from -6 to 6
- conv_w: bfloat16 [4, 27, 256, 256], P('section'), may hold values from -0.078125 to 0.078125
- proj_w: bfloat16 [4, 256, 256], P('section'), may hold values from -0.1875 to 0.1875
Outputs:
- section_grads: bfloat16 [4, 2, 4, 2, 8, 8, 256], P('section', None, 'dp', 'space')
- grad_conv: float32 [4, 256, 27, 256], P('section', 'dp')
- grad_proj: float32 [4, 256, 256], P('section', 'dp')
All inputs are finite; a program needn't handle non-finite values.
Results may differ from a plain program's by a relative error of at most 0.029.
Values may be sent and summed in bfloat16 or wider, within the bound.
No kernel may reach another device: no remote copies, remote signals or barrier semaphores. Data moves between devices by JAX's collectives and lax.ppermute only.
A program may use at most 64 MiB of HBM per device.

v0:
```python
import functools

import jax
import jax.numpy as jnp
from jax import lax
from jax.experimental import pallas as pl
from jax.experimental.pallas import tpu as pltpu
from jax.sharding import PartitionSpec as P

SIDE = (-1, 0, 1)
PLANE_TAPS = [(row, col) for row in SIDE for col in SIDE]
CONTRACT_LANES = (((1,), (1,)), ((), ()))
VMEM_LIMIT = 16 * 1024 * 1024


def peer(here, distance, count, back=False):
    if count & (count - 1) == 0:
        return here ^ distance
    return (here + (count - distance if back else distance)) % count


def neighbours(block, axis):
    count = lax.axis_size(axis)
    blocks = [block]
    for distance in range(1, count):
        pairs = [(peer(i, distance, count), i) for i in range(count)]
        blocks.append(lax.ppermute(block, axis, pairs))
    return blocks


def shifted(plane, row_off, col_off, height, width):
    lanes = plane.shape[1]
    step = row_off * width + col_off
    moved = pltpu.roll(plane, (-step) % lanes, 1) if step % lanes else plane
    place = lax.broadcasted_iota(jnp.int32, (1, lanes), 1)
    row = (place // width) % height + row_off
    col = place % width + col_off
    inside = (row >= 0) & (row < height) & (col >= 0) & (col < width)
    return jnp.where(inside, moved, jnp.zeros((), plane.dtype))


def block_step(grad, pre, conv_ref, proj, height, width):
    planes = len(grad)
    joined = jnp.concatenate(grad, axis=1)
    hidden_grad = jnp.dot(proj, joined, preferred_element_type=jnp.float32)
    keep = jnp.concatenate(pre, axis=1).astype(jnp.float32) > 0
    masked = jnp.where(keep, hidden_grad, 0.0).astype(jnp.bfloat16).astype(jnp.float32)
    lanes = grad[0].shape[1]
    total = joined.astype(jnp.float32)
    parts = [total[:, z * lanes : (z + 1) * lanes] for z in range(planes)]
    total = jnp.concatenate(parts, axis=1)
    taps = len(PLANE_TAPS)
    for tap, (row_off, col_off) in enumerate(PLANE_TAPS):
        moved = jnp.concatenate(
            [
                shifted(
                    masked[:, z * lanes : (z + 1) * lanes], -row_off, -col_off, height, width
                ).astype(jnp.bfloat16)
                for z in range(planes)
            ],
            axis=1,
        )
        blank = jnp.zeros((moved.shape[0], lanes), jnp.bfloat16)
        for depth, depth_off in enumerate(SIDE):
            if depth_off == 0:
                source = moved
            elif depth_off > 0:
                source = jnp.concatenate([blank, moved[:, : (planes - 1) * lanes]], axis=1)
            else:
                source = jnp.concatenate([moved[:, lanes:], blank], axis=1)
            total = total + jnp.dot(
                conv_ref[depth * taps + tap], source, preferred_element_type=jnp.float32
            )
    return [total[:, z * lanes : (z + 1) * lanes].astype(jnp.bfloat16) for z in range(planes)]


def flipped(rows):
    return rows.astype(jnp.float32).T


def prepare_kernel(seed_ref, pre_ref, acts_ref, conv_ref, proj_ref, *refs):
    seed_out, pre_out, acts_out, conv_out, proj_out, seed_rows, pre_rows, acts_rows, sems = refs
    rows_copies = [
        pltpu.make_async_copy(source, target, sems.at[place])
        for place, (source, target) in enumerate(
            ((seed_ref, seed_rows), (pre_ref, pre_rows), (acts_ref, acts_rows))
        )
    ]
    weight_copies = [
        pltpu.make_async_copy(conv_ref, conv_out, sems.at[3]),
        pltpu.make_async_copy(proj_ref, proj_out, sems.at[4]),
    ]
    for copy in rows_copies + weight_copies:
        copy.start()
    channels = seed_rows.shape[-1]
    for copy, rows, out in zip(
        rows_copies, (seed_rows, pre_rows, acts_rows), (seed_out, pre_out, acts_out)
    ):
        copy.wait()
        for depth in range(out.shape[0]):
            out[depth] = flipped(rows[:, depth].reshape(-1, channels)).astype(jnp.bfloat16)
    for copy in weight_copies:
        copy.wait()


def placed_planes(here, own_ref, row_refs, target):
    depth_dev, channels = own_ref.shape[:2]
    count = len(row_refs) + 1
    for depth in range(depth_dev):
        target[here * depth_dev + depth] = own_ref[depth].astype(target.dtype)
    for distance, rows_ref in enumerate(row_refs, 1):
        place = peer(here, distance, count)
        for depth in range(depth_dev):
            rows = rows_ref[:, depth].reshape(-1, channels)
            target[place * depth_dev + depth] = flipped(rows).astype(target.dtype)


def first_kernel(others, height, width, *refs):
    seed_ref, seed_rows = refs[0], refs[1 : 1 + others]
    pre_ref, pre_rows = refs[1 + others], refs[2 + others : 2 + 2 * others]
    conv_ref, proj_ref, grad_ref, pre_out_ref, out_ref = refs[2 + 2 * others :]
    here = lax.axis_index("space")
    placed_planes(here, seed_ref, seed_rows, grad_ref)
    placed_planes(here, pre_ref, pre_rows, pre_out_ref)
    step_kernel(0, height, width, grad_ref, pre_out_ref, conv_ref, proj_ref, out_ref)


def step_kernel(step, height, width, grad_ref, pre_ref, conv_ref, proj_ref, *refs):
    out_ref = refs[-1]
    planes = grad_ref.shape[0]

    @pl.when(lax.axis_index("section") == lax.axis_size("section") - 1 - step)
    def _():
        result = block_step(
            [grad_ref[z] for z in range(planes)],
            [pre_ref[z] for z in range(planes)],
            conv_ref,
            proj_ref[...],
            height,
            width,
        )
        for z in range(planes):
            out_ref[z] = result[z]


def pack_kernel(others, *refs):
    pre_ref, acts_ref, acts_rows = refs[0], refs[1], refs[2 : 2 + others]
    parcel_refs, scratch = refs[2 + others : -1], refs[-1]
    here = lax.axis_index("space")
    place = lax.axis_index("dp")
    count = len(parcel_refs)
    planes, channels = pre_ref.shape[:2]
    shard = channels // count
    padded = parcel_refs[0].shape[1] - channels
    placed_planes(here, acts_ref, acts_rows, scratch)
    for distance in range(count):
        target = peer(place, distance, count, back=True)
        for z in range(planes):
            parcel_refs[distance][z, :channels] = pre_ref[z]
            rows = scratch[z, pl.ds(pl.multiple_of(target * shard, shard), shard)]
            parcel_refs[distance][z, channels : channels + shard] = rows.astype(jnp.bfloat16)
            if padded > shard:
                parcel_refs[distance][z, channels + shard :] = jnp.zeros(
                    (padded - shard, rows.shape[1]), jnp.bfloat16
                )


def unfold_kernel(height, width, channels, shard, near, *refs):
    parcel_refs, near_ref, far_ref = refs[:-2], refs[-2], refs[-1]
    for place, parcel_ref in enumerate(parcel_refs):
        planes = [
            parcel_ref[z, channels:].astype(jnp.float32)[:shard]
            for z in range(parcel_ref.shape[0])
        ]
        moved = [
            [shifted(plane, row_off, col_off, height, width) for row_off, col_off in PLANE_TAPS]
            for plane in planes
        ]
        blank = jnp.zeros_like(planes[0])
        columns = []
        for z in range(len(planes)):
            taps = []
            for depth_off in SIDE:
                inside = 0 <= z + depth_off < len(planes)
                taps.extend(moved[z + depth_off] if inside else [blank] * len(PLANE_TAPS))
            columns.append(jnp.concatenate(taps, axis=0).astype(jnp.bfloat16))
        lanes = planes[0].shape[1] * len(planes)
        target, start = (near_ref, place) if place < near else (far_ref, place - near)
        target[:, start * lanes : (start + 1) * lanes] = jnp.concatenate(columns, axis=1)


def choose_kernel(count, *refs):
    step_refs, grad_ref = refs[:-1], refs[-1]
    section = lax.axis_index("section")
    for step, step_ref in enumerate(step_refs):

        @pl.when(section == count - 1 - step)
        def _(step_ref=step_ref):
            grad_ref[...] = step_ref[...]


def block_terms(grad_refs, parcel_refs, proj_ref, masked_ref, channels, shard):
    here = lax.axis_index("dp")
    total = None
    for place, (grad_ref, parcel_ref) in enumerate(zip(grad_refs, parcel_refs)):
        planes = grad_ref.shape[0]
        grad = jnp.concatenate([grad_ref[z] for z in range(planes)], axis=1)
        pre = jnp.concatenate([parcel_ref[z, :channels] for z in range(planes)], axis=1)
        hidden_grad = jnp.dot(proj_ref[...], grad, preferred_element_type=jnp.float32)
        lanes = grad.shape[1]
        masked_ref[:, place * lanes : (place + 1) * lanes] = jnp.where(
            pre.astype(jnp.float32) > 0, hidden_grad, 0.0
        ).astype(jnp.bfloat16)
        rows = pl.ds(pl.multiple_of(here * shard, shard), shard)
        mine = jnp.concatenate([parcel_ref[z, rows] for z in range(planes)], axis=1)
        hidden = jnp.maximum(mine.astype(jnp.float32), 0.0).astype(jnp.bfloat16)
        term = lax.dot_general(
            hidden, grad, CONTRACT_LANES, preferred_element_type=jnp.float32
        )
        total = term if total is None else total + term
    return total


def near_kernel(count, channels, shard, *refs):
    grad_refs, parcel_refs = refs[:count], refs[count : 2 * count]
    unfolded_ref, proj_ref, conv_out_ref, proj_out_ref, masked_ref = refs[2 * count :]
    proj_out_ref[...] = block_terms(
        grad_refs, parcel_refs, proj_ref, masked_ref, channels, shard
    )
    conv_out_ref[...] = lax.dot_general(
        unfolded_ref[...], masked_ref[...], CONTRACT_LANES, preferred_element_type=jnp.float32
    )


def far_kernel(count, channels, shard, scale_term, cuts, *refs):
    grad_refs, parcel_refs = refs[:count], refs[count : 2 * count]
    unfolded_ref, proj_ref, conv_near_ref, proj_near_ref = refs[2 * count : 2 * count + 4]
    conv_out_ref, proj_out_ref, masked_ref, rows_ref, sems = refs[2 * count + 4 :]
    proj_far = block_terms(grad_refs, parcel_refs, proj_ref, masked_ref, channels, shard)
    proj_out_ref[...] = (proj_near_ref[...] + proj_far) * scale_term
    size = rows_ref.shape[1]
    copies = []
    for cut in range(cuts):
        span = pl.ds(cut * size, size)
        total = conv_near_ref[span] + lax.dot_general(
            unfolded_ref[span], masked_ref[...], CONTRACT_LANES, preferred_element_type=jnp.float32
        )
        rows_ref[cut] = total * scale_term
        copies.append(
            pltpu.make_async_copy(rows_ref.at[cut], conv_out_ref.at[span], sems.at[cut])
        )
        copies[-1].start()
    for copy in copies:
        copy.wait()


def select_kernel(count, depth_dev, *refs):
    out_refs, section_ref = refs[:count], refs[count]
    section = lax.axis_index("section")
    here = lax.axis_index("space")
    micro, _, area, channels = section_ref.shape
    for step in range(count):

        @pl.when(section == count - 1 - step)
        def _(step=step):
            for depth in range(depth_dev):
                plane = out_refs[step][here * depth_dev + depth].astype(jnp.float32)
                rows = plane.T.astype(jnp.bfloat16)
                for index in range(micro):
                    section_ref[index, depth] = rows[index * area : (index + 1) * area]


def whole(count=1):
    return [pl.BlockSpec(memory_space=pltpu.VMEM)] * count


def params():
    return pltpu.CompilerParams(vmem_limit_bytes=VMEM_LIMIT)


def kept_in_hbm(*arrays):
    return [pltpu.with_memory_space_constraint(array, pltpu.HBM) for array in arrays]


def shards(inputs, preacts, out_grad, conv_w, proj_w):
    section_count = lax.axis_size("section")
    crop_count = lax.axis_size("dp")
    space_count = lax.axis_size("space")
    micro, _, depth_dev, height, width, channels = inputs.shape[1:]
    area = height * width
    lanes = micro * area
    planes = space_count * depth_dev
    taps = len(SIDE) * len(PLANE_TAPS)
    shard = channels // crop_count
    others = space_count - 1
    scale_term = 1.0 / (micro * crop_count)
    local = (micro, depth_dev, area, channels)
    acts = inputs.reshape(local)
    pre_acts = preacts.reshape(local)
    seeds = out_grad.reshape(local)
    bfloat = jnp.bfloat16
    volume = jax.ShapeDtypeStruct((planes, channels, lanes), bfloat)
    slab = jax.ShapeDtypeStruct((depth_dev, channels, lanes), bfloat)
    padded = -(-shard // 16) * 16
    parcel = jax.ShapeDtypeStruct((planes, channels + padded, lanes), bfloat)

    seed_rows = neighbours(seeds, "space")[1:]
    pre_rows = neighbours(pre_acts, "space")[1:]
    acts_rows = neighbours(acts, "space")[1:]

    seed_own, pre_own, acts_own, conv_weight, proj_weight = pl.pallas_call(
        prepare_kernel,
        out_shape=(
            slab,
            slab,
            slab,
            jax.ShapeDtypeStruct(conv_w.shape[1:], bfloat),
            jax.ShapeDtypeStruct(proj_w.shape[1:], bfloat),
        ),
        in_specs=[pl.BlockSpec(memory_space=pltpu.HBM)] * 5,
        out_specs=tuple(whole(5)),
        scratch_shapes=[pltpu.VMEM(local, bfloat)] * 3 + [pltpu.SemaphoreType.DMA((5,))],
        compiler_params=params(),
        name="prepare",
    )(*kept_in_hbm(seeds, pre_acts, acts, conv_w[0], proj_w[0]))

    grad_first, pre_all, result = pl.pallas_call(
        functools.partial(first_kernel, others, height, width),
        out_shape=(volume, volume, volume),
        in_specs=whole(4 + 2 * others),
        out_specs=tuple(whole(3)),
        compiler_params=params(),
        name="first_block",
    )(seed_own, *seed_rows, pre_own, *pre_rows, conv_weight, proj_weight)

    results = [result]
    received = []
    parcels = None
    for step in range(1, section_count):
        senders = section_count + 1 - step
        ring = [((i + 1) % senders, i) for i in range(senders)]
        received.append(lax.ppermute(results[-1], "section", ring))
        if parcels is None:
            sent = pl.pallas_call(
                functools.partial(pack_kernel, others),
                out_shape=(parcel,) * crop_count,
                in_specs=whole(2 + others),
                out_specs=tuple(whole(crop_count)),
                scratch_shapes=[pltpu.VMEM(volume.shape, jnp.float32)],
                compiler_params=params(),
                name="pack",
            )(pre_all, acts_own, *acts_rows)
            parcels = [sent[0]] + [
                lax.ppermute(
                    sent[distance],
                    "dp",
                    [(peer(i, distance, crop_count), i) for i in range(crop_count)],
                )
                for distance in range(1, crop_count)
            ]
        step_call = pl.pallas_call(
            functools.partial(step_kernel, step, height, width),
            out_shape=volume,
            in_specs=whole(4) + [pl.BlockSpec(memory_space=pl.ANY)],
            out_specs=whole()[0],
            compiler_params=params(),
            name="block",
        )
        results.append(step_call(received[-1], pre_all, conv_weight, proj_weight, parcels[0]))
    grad_own = pl.pallas_call(
        functools.partial(choose_kernel, section_count),
        out_shape=volume,
        in_specs=whole(section_count),
        out_specs=whole()[0],
        compiler_params=params(),
        name="choose",
    )(grad_first, *received)
    grad_blocks = neighbours(grad_own, "dp")

    near = crop_count // 2
    span = planes * lanes
    near_unfolded, far_unfolded = pl.pallas_call(
        functools.partial(unfold_kernel, height, width, channels, shard, near),
        out_shape=(
            jax.ShapeDtypeStruct((taps * shard, near * span), bfloat),
            jax.ShapeDtypeStruct((taps * shard, (crop_count - near) * span), bfloat),
        ),
        in_specs=whole(crop_count),
        out_specs=tuple(whole(2)),
        compiler_params=params(),
        name="unfold",
    )(*parcels)

    conv_shape = jax.ShapeDtypeStruct((taps * shard, channels), jnp.float32)
    proj_shape = jax.ShapeDtypeStruct((shard, channels), jnp.float32)
    conv_near, proj_near = pl.pallas_call(
        functools.partial(near_kernel, near, channels, shard),
        out_shape=(conv_shape, proj_shape),
        in_specs=whole(2 * near + 2),
        out_specs=tuple(whole(2)),
        scratch_shapes=[pltpu.VMEM((channels, near * span), bfloat)],
        compiler_params=params(),
        name="near_weight_grads",
    )(*grad_blocks[:near], *parcels[:near], near_unfolded, proj_weight)

    cuts = len(SIDE) if (len(PLANE_TAPS) * shard) % 16 == 0 else 1
    far = crop_count - near
    conv_rows, proj_rows = pl.pallas_call(
        functools.partial(far_kernel, far, channels, shard, scale_term, cuts),
        out_shape=(conv_shape, proj_shape),
        in_specs=whole(2 * far + 4),
        out_specs=(pl.BlockSpec(memory_space=pltpu.HBM), whole()[0]),
        scratch_shapes=[
            pltpu.VMEM((channels, far * span), bfloat),
            pltpu.VMEM((cuts, taps * shard // cuts, channels), jnp.float32),
            pltpu.SemaphoreType.DMA((cuts,)),
        ],
        compiler_params=params(),
        name="far_weight_grads",
    )(*grad_blocks[near:], *parcels[near:], far_unfolded, proj_weight, conv_near, proj_near)

    section_out = pl.pallas_call(
        functools.partial(select_kernel, section_count, depth_dev),
        out_shape=jax.ShapeDtypeStruct(local, bfloat),
        in_specs=whole(section_count),
        out_specs=whole()[0],
        compiler_params=params(),
        name="own_grads",
    )(*results)

    section_grads = section_out.reshape(inputs.shape)
    grad_conv = conv_rows.reshape(taps, shard, channels).swapaxes(0, 1)[None]
    return section_grads, grad_conv, proj_rows[None]


def solution(mesh):
    placed = (
        P("section", None, "dp", "space", None, None, None),
        P("section", None, "dp", "space", None, None, None),
        P(None, "dp", "space", None, None, None),
        P("section", None, None, None),
        P("section", None, None),
    )
    return jax.shard_map(
        shards,
        mesh=mesh,
        in_specs=placed,
        out_specs=(
            P("section", None, "dp", "space", None, None, None),
            P("section", "dp", None, None),
            P("section", "dp", None),
        ),
        check_vma=False,
    )
```

profile of v0, /device:TPU:0, one launch (start us, length us, event | category | flops | bytes accessed | tf_op | source)
XLA Modules:
  0.0 42.6 jit_solution(14741700039519440665)
XLA Ops:
  0.6 3.0 %collective-permute-start.1 = (bf16[2,1,64,256]{3,2,1,0:T(8,128)(2,1)}, bf16[2,1,64,256]{3,2,1,0:T(8,128)(2,1)S(1)}, u32[]{:S(2)}, u32[]{:S(2)}) collective-permute-start(bf16[2,1,64,256]{3,2,1,0:T(8,128)(2,1)} %bitcast.16), channel_id=1, source_target_pairs={{1,0},{0,1},{3,2},{2,3},{5,4},{4,5},{7,6},{6,7},{9,8},{8,9},{11,10... | collective-permute-start | bytes 196616 | tf_op jit(solution)/shard_map/ppermute | solution.py:27
  3.7 0.1 collective-permute-start
  3.7 2.2 %prepare.1 = (bf16[1,256,128]{2,1,0:T(8,128)(2,1)S(1)}, bf16[1,256,128]{2,1,0:T(8,128)(2,1)S(1)}, bf16[1,256,128]{2,1,0:T(8,128)(2,1)S(1)}, bf16[27,256,256]{2,1,0:T(8,128)(2,1)S(1)}, bf16[256,256]{1,0:T(8,128)(2,1)S(1)}) custom-call(bf16[2,1,64,256]{3,2,1,0:T(8,128)(2,1)} %bitcast.19, bf16[2,1,64,256]{3,2,1,0:T(8,128)(2,1)} %bitcast.17, ...), custom_call_target="tpu_custom_call" | custom-call | tf_op jit(solution)/shard_map/prepare/pallas_call | solution.py:311
  5.9 0.4 collective-permute-done.1.refs_3_
  6.3 1.9 %collective-permute-done.refs_1_ = bf16[2,1,64,256]{3,2,1,0:T(8,128)(2,1)S(1)} collective-permute-done((bf16[2,1,64,256]{3,2,1,0:T(8,128)(2,1)}, bf16[2,1,64,256]{3,2,1,0:T(8,128)(2,1)S(1)}, u32[]{:S(2)}, u32[]{:S(2)}) %collective-permute-start) | collective-permute-done | bytes 65568 | tf_op jit(solution)/shard_map/ppermute | solution.py:27
  8.1 0.0 copy-start
  8.1 0.1 first_block.1
  8.3 5.0 %collective-permute-start.2 = (bf16[2,256,128]{2,1,0:T(8,128)(2,1)S(1)}, bf16[2,256,128]{2,1,0:T(8,128)(2,1)S(1)}, u32[]{:S(2)}, u32[]{:S(2)}) collective-permute-start(bf16[2,256,128]{2,1,0:T(8,128)(2,1)S(1)} %get-tuple-element.25.refs_0_), channel_id=1, source_target_pairs={{8,0},{16,8},{24,16},{0,24},{9,1},{17,9},{25,17},{1,25},{10,2},{18... | collective-permute-start | bytes 393224 | tf_op jit(solution)/shard_map/ppermute | solution.py:342
  13.3 0.0 copy-done
  13.3 1.0 %collective-permute-start.3 = (bf16[2,1,64,256]{3,2,1,0:T(8,128)(2,1)S(1)}, bf16[2,1,64,256]{3,2,1,0:T(8,128)(2,1)S(1)}, u32[]{:S(2)}, u32[]{:S(2)}) collective-permute-start(bf16[2,1,64,256]{3,2,1,0:T(8,128)(2,1)S(1)} %bitcast.21), channel_id=1, source_target_pairs={{1,0},{0,1},{3,2},{2,3},{5,4},{4,5},{7,6},{6,7},{9,8},{8,9},{11,10... | collective-permute-start | bytes 196616 | tf_op jit(solution)/shard_map/ppermute | solution.py:27
  14.2 3.3 %collective-permute-done.3.refs_2_ = bf16[2,1,64,256]{3,2,1,0:T(8,128)(2,1)S(1)} collective-permute-done((bf16[2,1,64,256]{3,2,1,0:T(8,128)(2,1)S(1)}, bf16[2,1,64,256]{3,2,1,0:T(8,128)(2,1)S(1)}, u32[]{:S(2)}, u32[]{:S(2)}) %collective-permute-start.3) | collective-permute-done | bytes 65568 | tf_op jit(solution)/shard_map/ppermute | solution.py:27
  17.5 0.1 pack.1
  17.7 0.0 collective-permute-done.2.grad_ref.refs_1_
  17.7 2.4 %collective-permute-start.4 = (bf16[2,256,128]{2,1,0:T(8,128)(2,1)S(1)}, bf16[2,256,128]{2,1,0:T(8,128)(2,1)S(1)}, u32[]{:S(2)}, u32[]{:S(2)}) collective-permute-start(bf16[2,256,128]{2,1,0:T(8,128)(2,1)S(1)} %block.3.refs_1_), channel_id=1, source_target_pairs={{8,0},{16,8},{0,16},{9,1},{17,9},{1,17},{10,2},{18,10},{2,18},{11,... | collective-permute-start | bytes 393224 | tf_op jit(solution)/shard_map/ppermute | solution.py:342
  20.1 1.6 %collective-permute-start.8 = (bf16[2,320,128]{2,1,0:T(8,128)(2,1)S(1)}, bf16[2,320,128]{2,1,0:T(8,128)(2,1)S(1)}, u32[]{:S(2)}, u32[]{:S(2)}) collective-permute-start(bf16[2,320,128]{2,1,0:T(8,128)(2,1)S(1)} %get-tuple-element.30), channel_id=1, source_target_pairs={{4,0},{6,2},{0,4},{2,6},{5,1},{7,3},{1,5},{3,7},{12,8},{14,10},{8,... | collective-permute-start | bytes 491528 | tf_op jit(solution)/shard_map/ppermute | solution.py:354
  21.6 2.9 %collective-permute-done.4.grad_ref.refs_2_ = bf16[2,256,128]{2,1,0:T(8,128)(2,1)S(1)} collective-permute-done((bf16[2,256,128]{2,1,0:T(8,128)(2,1)S(1)}, bf16[2,256,128]{2,1,0:T(8,128)(2,1)S(1)}, u32[]{:S(2)}, u32[]{:S(2)}) %collective-permute-start.4) | collective-permute-done | bytes 131104 | tf_op jit(solution)/shard_map/ppermute | solution.py:342
  24.6 2.9 %collective-permute-start.5 = (bf16[2,256,128]{2,1,0:T(8,128)(2,1)S(1)}, bf16[2,256,128]{2,1,0:T(8,128)(2,1)S(1)}, u32[]{:S(2)}, u32[]{:S(2)}) collective-permute-start(bf16[2,256,128]{2,1,0:T(8,128)(2,1)S(1)} %block.4.refs_2_), channel_id=1, source_target_pairs={{8,0},{0,8},{9,1},{1,9},{10,2},{2,10},{11,3},{3,11},{12,4},{4,12},... | collective-permute-start | bytes 393224 | tf_op jit(solution)/shard_map/ppermute | solution.py:342
  27.4 0.1 collective-permute-start.9
  27.5 1.6 %collective-permute-start.10 = (bf16[2,320,128]{2,1,0:T(8,128)(2,1)S(1)}, bf16[2,320,128]{2,1,0:T(8,128)(2,1)S(1)}, u32[]{:S(2)}, u32[]{:S(2)}) collective-permute-start(bf16[2,320,128]{2,1,0:T(8,128)(2,1)S(1)} %get-tuple-element.32), channel_id=1, source_target_pairs={{2,0},{0,2},{6,4},{4,6},{3,1},{1,3},{7,5},{5,7},{10,8},{8,10},{14,... | collective-permute-start | bytes 491528 | tf_op jit(solution)/shard_map/ppermute | solution.py:354
  29.1 2.3 %collective-permute-done.5.grad_ref.refs_3_ = bf16[2,256,128]{2,1,0:T(8,128)(2,1)S(1)} collective-permute-done((bf16[2,256,128]{2,1,0:T(8,128)(2,1)S(1)}, bf16[2,256,128]{2,1,0:T(8,128)(2,1)S(1)}, u32[]{:S(2)}, u32[]{:S(2)}) %collective-permute-start.5) | collective-permute-done | bytes 131104 | tf_op jit(solution)/shard_map/ppermute | solution.py:342
  31.4 0.1 collective-permute-start.11
  31.5 1.6 %collective-permute-start.7 = (bf16[2,256,128]{2,1,0:T(8,128)(2,1)S(1)}, bf16[2,256,128]{2,1,0:T(8,128)(2,1)S(1)}, u32[]{:S(2)}, u32[]{:S(2)}) collective-permute-start(bf16[2,256,128]{2,1,0:T(8,128)(2,1)S(1)} %choose.1.refs_0_), channel_id=1, source_target_pairs={{6,0},{4,2},{2,4},{0,6},{7,1},{5,3},{3,5},{1,7},{14,8},{12,10},{10... | collective-permute-start | bytes 393224 | tf_op jit(solution)/shard_map/ppermute | solution.py:27
  33.1 0.0 collective-permute-done.8.refs_2_
  33.1 0.5 %collective-permute-start.6 = (bf16[2,256,128]{2,1,0:T(8,128)(2,1)S(1)}, bf16[2,256,128]{2,1,0:T(8,128)(2,1)S(1)}, u32[]{:S(2)}, u32[]{:S(2)}) collective-permute-start(bf16[2,256,128]{2,1,0:T(8,128)(2,1)S(1)} %choose.1.refs_0_), channel_id=1, source_target_pairs={{4,0},{6,2},{0,4},{2,6},{5,1},{7,3},{1,5},{3,7},{12,8},{14,10},{8,... | collective-permute-start | bytes 393224 | tf_op jit(solution)/shard_map/ppermute | solution.py:27
  33.7 0.3 collective-permute-done.9.refs_3_
  33.9 0.0 collective-permute-done.10.refs_1_.refs_3_
  33.9 0.4 unfold.1
  34.3 1.4 %block.5.refs_3_ = bf16[2,256,128]{2,1,0:T(8,128)(2,1)S(1)} custom-call(bf16[2,256,128]{2,1,0:T(8,128)(2,1)S(1)} %collective-permute-done.5.grad_ref.refs_3_, bf16[2,256,128]{2,1,0:T(8,128)(2,1)S(1)} %get-tuple-element.26.refs_0_.pre_ref, bf16[27,256,256]{2,1,0:T(8,128)(2,1)S(1)} %get-tuple-element.23.refs_4_.conv_ref, ...), custom_call_target="tpu_custom_call" | custom-call | tf_op jit(solution)/shard_map/block/pallas_call | solution.py:369
  35.7 0.8 %own_grads.1 = bf16[2,1,64,256]{3,2,1,0:T(8,128)(2,1)} custom-call(bf16[2,256,128]{2,1,0:T(8,128)(2,1)S(1)} %get-tuple-element.25.refs_0_, bf16[2,256,128]{2,1,0:T(8,128)(2,1)S(1)} %block.3.refs_1_, bf16[2,256,128]{2,1,0:T(8,128)(2,1)S(1)} %block.4.refs_2_, bf16[2,256,128]{2,1,0:T(8,128)(2,1)S(1)} %block.5.refs_3_), custom_call_target="tpu_custom_call" | custom-call | tf_op jit(solution)/shard_map/own_grads/pallas_call | solution.py:422
  36.5 0.0 collective-permute-done.11.refs_1_
  36.5 0.9 %near_weight_grads.1 = (f32[1728,256]{1,0:T(8,128)S(1)}, f32[64,256]{1,0:T(8,128)S(1)}) custom-call(bf16[2,256,128]{2,1,0:T(8,128)(2,1)S(1)} %choose.1.refs_0_, bf16[2,256,128]{2,1,0:T(8,128)(2,1)S(1)} %collective-permute-done.11.refs_1_, bf16[2,320,128]{2,1,0:T(8,128)(2,1)S(1)} %get-tuple-element.28.refs_0_.refs_2_, ...), custom_call_target="tpu_custom_call" | custom-call | tf_op jit(solution)/shard_map/near_weight_grads/pallas_call | solution.py:396
  37.4 0.0 collective-permute-done.7.refs_1_
  37.4 2.8 %collective-permute-done.6.refs_0_ = bf16[2,256,128]{2,1,0:T(8,128)(2,1)S(1)} collective-permute-done((bf16[2,256,128]{2,1,0:T(8,128)(2,1)S(1)}, bf16[2,256,128]{2,1,0:T(8,128)(2,1)S(1)}, u32[]{:S(2)}, u32[]{:S(2)}) %collective-permute-start.6) | collective-permute-done | bytes 131104 | tf_op jit(solution)/shard_map/ppermute | solution.py:27
  40.2 2.5 %far_weight_grads.1 = (f32[1728,256]{1,0:T(8,128)}, f32[64,256]{1,0:T(8,128)}) custom-call(bf16[2,256,128]{2,1,0:T(8,128)(2,1)S(1)} %collective-permute-done.6.refs_0_, bf16[2,256,128]{2,1,0:T(8,128)(2,1)S(1)} %collective-permute-done.7.refs_1_, bf16[2,320,128]{2,1,0:T(8,128)(2,1)S(1)} %collective-permute-done.8.refs_2_, ...), custom_call_target="tpu_custom_call" | custom-call | tf_op jit(solution)/shard_map/far_weight_grads/pallas_call | solution.py:408
  (3 shorter events, 0.0 us)
Async XLA Ops:
  0.6 5.6 %collective-permute-start.1 = (bf16[2,1,64,256]{3,2,1,0:T(8,128)(2,1)}, bf16[2,1,64,256]{3,2,1,0:T(8,128)(2,1)S(1)}, u32[]{:S(2)}, u32[]{:S(2)}) collective-permute-start(bf16[2,1,64,256]{3,2,1,0:T(8,128)(2,1)} %bitcast.16), channel_id=1, source_target_pairs={{1,0},{0,1},{3,2},{2,3},{5,4},{4,5},{7,6},{6,7},{9,8},{8,9},{11,10... | collective-permute-start | bytes 196616 | tf_op jit(solution)/shard_map/ppermute | solution.py:27
  3.7 4.5 %collective-permute-start = (bf16[2,1,64,256]{3,2,1,0:T(8,128)(2,1)}, bf16[2,1,64,256]{3,2,1,0:T(8,128)(2,1)S(1)}, u32[]{:S(2)}, u32[]{:S(2)}) collective-permute-start(bf16[2,1,64,256]{3,2,1,0:T(8,128)(2,1)} %bitcast.18), channel_id=1, source_target_pairs={{1,0},{0,1},{3,2},{2,3},{5,4},{4,5},{7,6},{6,7},{9,8},{8,9},{11,10... | collective-permute-start | bytes 196616 | tf_op jit(solution)/shard_map/ppermute | solution.py:27
  8.1 5.1 %copy-start = (bf16[1,2,1,1,8,8,256]{6,5,4,3,2,1,0:T(8,128)(2,1)S(1)}, bf16[1,2,1,1,8,8,256]{6,5,4,3,2,1,0:T(8,128)(2,1)}, u32[]{:S(2)}) copy-start(bf16[1,2,1,1,8,8,256]{6,5,4,3,2,1,0:T(8,128)(2,1)} %param.5) | copy-start | bytes 196612
  8.3 9.4 %collective-permute-start.2 = (bf16[2,256,128]{2,1,0:T(8,128)(2,1)S(1)}, bf16[2,256,128]{2,1,0:T(8,128)(2,1)S(1)}, u32[]{:S(2)}, u32[]{:S(2)}) collective-permute-start(bf16[2,256,128]{2,1,0:T(8,128)(2,1)S(1)} %get-tuple-element.25.refs_0_), channel_id=1, source_target_pairs={{8,0},{16,8},{24,16},{0,24},{9,1},{17,9},{25,17},{1,25},{10,2},{18... | collective-permute-start | bytes 393224 | tf_op jit(solution)/shard_map/ppermute | solution.py:342
  13.3 4.3 %collective-permute-start.3 = (bf16[2,1,64,256]{3,2,1,0:T(8,128)(2,1)S(1)}, bf16[2,1,64,256]{3,2,1,0:T(8,128)(2,1)S(1)}, u32[]{:S(2)}, u32[]{:S(2)}) collective-permute-start(bf16[2,1,64,256]{3,2,1,0:T(8,128)(2,1)S(1)} %bitcast.21), channel_id=1, source_target_pairs={{1,0},{0,1},{3,2},{2,3},{5,4},{4,5},{7,6},{6,7},{9,8},{8,9},{11,10... | collective-permute-start | bytes 196616 | tf_op jit(solution)/shard_map/ppermute | solution.py:27
  17.7 6.9 %collective-permute-start.4 = (bf16[2,256,128]{2,1,0:T(8,128)(2,1)S(1)}, bf16[2,256,128]{2,1,0:T(8,128)(2,1)S(1)}, u32[]{:S(2)}, u32[]{:S(2)}) collective-permute-start(bf16[2,256,128]{2,1,0:T(8,128)(2,1)S(1)} %block.3.refs_1_), channel_id=1, source_target_pairs={{8,0},{16,8},{0,16},{9,1},{17,9},{1,17},{10,2},{18,10},{2,18},{11,... | collective-permute-start | bytes 393224 | tf_op jit(solution)/shard_map/ppermute | solution.py:342
  20.1 13.0 %collective-permute-start.8 = (bf16[2,320,128]{2,1,0:T(8,128)(2,1)S(1)}, bf16[2,320,128]{2,1,0:T(8,128)(2,1)S(1)}, u32[]{:S(2)}, u32[]{:S(2)}) collective-permute-start(bf16[2,320,128]{2,1,0:T(8,128)(2,1)S(1)} %get-tuple-element.30), channel_id=1, source_target_pairs={{4,0},{6,2},{0,4},{2,6},{5,1},{7,3},{1,5},{3,7},{12,8},{14,10},{8,... | collective-permute-start | bytes 491528 | tf_op jit(solution)/shard_map/ppermute | solution.py:354
  24.6 6.8 %collective-permute-start.5 = (bf16[2,256,128]{2,1,0:T(8,128)(2,1)S(1)}, bf16[2,256,128]{2,1,0:T(8,128)(2,1)S(1)}, u32[]{:S(2)}, u32[]{:S(2)}) collective-permute-start(bf16[2,256,128]{2,1,0:T(8,128)(2,1)S(1)} %block.4.refs_2_), channel_id=1, source_target_pairs={{8,0},{0,8},{9,1},{1,9},{10,2},{2,10},{11,3},{3,11},{12,4},{4,12},... | collective-permute-start | bytes 393224 | tf_op jit(solution)/shard_map/ppermute | solution.py:342
  27.4 6.5 %collective-permute-start.9 = (bf16[2,320,128]{2,1,0:T(8,128)(2,1)S(1)}, bf16[2,320,128]{2,1,0:T(8,128)(2,1)S(1)}, u32[]{:S(2)}, u32[]{:S(2)}) collective-permute-start(bf16[2,320,128]{2,1,0:T(8,128)(2,1)S(1)} %get-tuple-element.31), channel_id=1, source_target_pairs={{6,0},{4,2},{2,4},{0,6},{7,1},{5,3},{3,5},{1,7},{14,8},{12,10},{10... | collective-permute-start | bytes 491528 | tf_op jit(solution)/shard_map/ppermute | solution.py:354
  27.5 6.4 %collective-permute-start.10 = (bf16[2,320,128]{2,1,0:T(8,128)(2,1)S(1)}, bf16[2,320,128]{2,1,0:T(8,128)(2,1)S(1)}, u32[]{:S(2)}, u32[]{:S(2)}) collective-permute-start(bf16[2,320,128]{2,1,0:T(8,128)(2,1)S(1)} %get-tuple-element.32), channel_id=1, source_target_pairs={{2,0},{0,2},{6,4},{4,6},{3,1},{1,3},{7,5},{5,7},{10,8},{8,10},{14,... | collective-permute-start | bytes 491528 | tf_op jit(solution)/shard_map/ppermute | solution.py:354
  31.4 5.0 %collective-permute-start.11 = (bf16[2,256,128]{2,1,0:T(8,128)(2,1)S(1)}, bf16[2,256,128]{2,1,0:T(8,128)(2,1)S(1)}, u32[]{:S(2)}, u32[]{:S(2)}) collective-permute-start(bf16[2,256,128]{2,1,0:T(8,128)(2,1)S(1)} %choose.1.refs_0_), channel_id=1, source_target_pairs={{2,0},{0,2},{6,4},{4,6},{3,1},{1,3},{7,5},{5,7},{10,8},{8,10},{14,... | collective-permute-start | bytes 393224 | tf_op jit(solution)/shard_map/ppermute | solution.py:27
  31.5 5.8 %collective-permute-start.7 = (bf16[2,256,128]{2,1,0:T(8,128)(2,1)S(1)}, bf16[2,256,128]{2,1,0:T(8,128)(2,1)S(1)}, u32[]{:S(2)}, u32[]{:S(2)}) collective-permute-start(bf16[2,256,128]{2,1,0:T(8,128)(2,1)S(1)} %choose.1.refs_0_), channel_id=1, source_target_pairs={{6,0},{4,2},{2,4},{0,6},{7,1},{5,3},{3,5},{1,7},{14,8},{12,10},{10... | collective-permute-start | bytes 393224 | tf_op jit(solution)/shard_map/ppermute | solution.py:27
  33.1 7.1 %collective-permute-start.6 = (bf16[2,256,128]{2,1,0:T(8,128)(2,1)S(1)}, bf16[2,256,128]{2,1,0:T(8,128)(2,1)S(1)}, u32[]{:S(2)}, u32[]{:S(2)}) collective-permute-start(bf16[2,256,128]{2,1,0:T(8,128)(2,1)S(1)} %choose.1.refs_0_), channel_id=1, source_target_pairs={{4,0},{6,2},{0,4},{2,6},{5,1},{7,3},{1,5},{3,7},{12,8},{14,10},{8,... | collective-permute-start | bytes 393224 | tf_op jit(solution)/shard_map/ppermute | solution.py:27
where the time goes:
time: 42.8 us; the launch traced here: 42.6 us
  starting transfers between devices  19.8 us (46%)
  waiting for transfers between devices  13.9 us (32%)
  Pallas kernels  8.25 us (19%)
  between operations  0.73 us (2%)
    ppermute x3, starting transfers between devices, shards(): received.append(lax.ppermute(results[-1], 'section', ring))  10.2 us
    ppermute x6, waiting for transfers between devices, neighbours(): blocks.append(lax.ppermute(block, axis, pairs))  8.34 us
    ppermute x6, starting transfers between devices, neighbours(): blocks.append(lax.ppermute(block, axis, pairs))  6.29 us
    ppermute x3, waiting for transfers between devices, shards(): received.append(lax.ppermute(results[-1], 'section', ring))  5.25 us
    ppermute x3, starting transfers between devices, shards(): lax.ppermute(sent[distance], 'dp', [(peer(i, distance, crop_count), i) fo...  3.22 us
    pallas_call x1, Pallas kernels, shards(): pl.pallas_call(functools.partial(far_kernel, far, channels, shard, scale_...  2.45 us
    pallas_call x1, Pallas kernels, shards(): pl.pallas_call(prepare_kernel, out_shape=(slab, slab, slab, jax.ShapeDtyp...  2.16 us
    pallas_call x3, Pallas kernels, shards(): step_call(received[-1], pre_all, conv_weight, proj_weight, parcels[0])  1.4 us
  transfers between devices with their start and end apart: 12, of which 7 were waited for; matrix products, arithmetic and copies ran while one was open for 0% of the time, Pallas kernels for 13%

commit v1 on v0

--- a/solution.py
+++ b/solution.py
@@ -26,6 +26,14 @@
         pairs = [(peer(i, distance, count), i) for i in range(count)]
         blocks.append(lax.ppermute(block, axis, pairs))
     return blocks
+
+
+def hop_pairs(count, step):
+    if step == 1:
+        return [((i + 1) % count, i) for i in range(count)]
+    sender = count - step
+    swapped = {sender: sender - 1, sender - 1: sender}
+    return [(i, swapped.get(i, i)) for i in range(count)]
 
 
 def shifted(plane, row_off, col_off, height, width):
@@ -337,9 +345,7 @@
     received = []
     parcels = None
     for step in range(1, section_count):
-        senders = section_count + 1 - step
-        ring = [((i + 1) % senders, i) for i in range(senders)]
-        received.append(lax.ppermute(results[-1], "section", ring))
+        received.append(lax.ppermute(results[-1], "section", hop_pairs(section_count, step)))
         if parcels is None:
             sent = pl.pallas_call(
                 functools.partial(pack_kernel, others),

time: 42.8 us -> 41.7 us (0.974)
  waiting for transfers between devices: 13.9 us -> 10.4 us
  starting transfers between devices: 19.8 us -> 22.1 us
    ppermute x3, waiting for transfers between devices: 5.25 us -> 1.26 us  [shards(): lax.ppermute(results[-1], 'section', hop_pairs(section_count, step))]
    ppermute x3, starting transfers between devices: 10.2 us -> 12.6 us  [shards(): lax.ppermute(results[-1], 'section', hop_pairs(section_count, step))]
    ppermute x3, waiting for transfers between devices: 0.29 us -> 1.35 us  [shards(): lax.ppermute(sent[distance], 'dp', [(peer(i, distance, crop_count), i) fo...]
    ppermute x6, waiting for transfers between devices: 8.34 us -> 7.77 us  [neighbours(): blocks.append(lax.ppermute(block, axis, pairs))]
  transfers between devices with their start and end apart: 12 -> 12, of which waited for: 7 -> 6; matrix products, arithmetic and copies ran while one was open for 0% -> 0% of each run, Pallas kernels for 13% -> 14%
where the time goes in v1:
time: 41.7 us; the launch traced here: 41.5 us
  starting transfers between devices  22.1 us (53%)
  waiting for transfers between devices  10.4 us (25%)
  Pallas kernels  8.25 us (20%)
  between operations  0.73 us (2%)
    ppermute x3, starting transfers between devices, shards(): lax.ppermute(results[-1], 'section', hop_pairs(section_count, step))  12.6 us
    ppermute x6, waiting for transfers between devices, neighbours(): blocks.append(lax.ppermute(block, axis, pairs))  7.77 us
    ppermute x6, starting transfers between devices, neighbours(): blocks.append(lax.ppermute(block, axis, pairs))  6.29 us
    ppermute x3, starting transfers between devices, shards(): lax.ppermute(sent[distance], 'dp', [(peer(i, distance, crop_count), i) fo...  3.22 us
    pallas_call x1, Pallas kernels, shards(): pl.pallas_call(functools.partial(far_kernel, far, channels, shard, scale_...  2.45 us
    pallas_call x1, Pallas kernels, shards(): pl.pallas_call(prepare_kernel, out_shape=(slab, slab, slab, jax.ShapeDtyp...  2.16 us
    pallas_call x3, Pallas kernels, shards(): step_call(received[-1], pre_all, conv_weight, proj_weight, parcels[0])  1.4 us
    ppermute x3, waiting for transfers between devices, shards(): lax.ppermute(sent[distance], 'dp', [(peer(i, distance, crop_count), i) fo...  1.35 us
  transfers between devices with their start and end apart: 12, of which 6 were waited for; matrix products, arithmetic and copies ran while one was open for 0% of the time, Pallas kernels for 14%

profile of v1, /device:TPU:0, one launch (start us, length us, event | category | flops | bytes accessed | tf_op | source)
XLA Modules:
  0.0 41.5 jit_solution(13078774516294725073)
XLA Ops:
  0.6 3.0 %collective-permute-start.1 = (bf16[2,1,64,256]{3,2,1,0:T(8,128)(2,1)}, bf16[2,1,64,256]{3,2,1,0:T(8,128)(2,1)S(1)}, u32[]{:S(2)}, u32[]{:S(2)}) collective-permute-start(bf16[2,1,64,256]{3,2,1,0:T(8,128)(2,1)} %bitcast.16), channel_id=1, source_target_pairs={{1,0},{0,1},{3,2},{2,3},{5,4},{4,5},{7,6},{6,7},{9,8},{8,9},{11,10... | collective-permute-start | bytes 196616 | tf_op jit(solution)/shard_map/ppermute | solution.py:27
  3.7 0.1 collective-permute-start
  3.7 2.2 %prepare.1 = (bf16[1,256,128]{2,1,0:T(8,128)(2,1)S(1)}, bf16[1,256,128]{2,1,0:T(8,128)(2,1)S(1)}, bf16[1,256,128]{2,1,0:T(8,128)(2,1)S(1)}, bf16[27,256,256]{2,1,0:T(8,128)(2,1)S(1)}, bf16[256,256]{1,0:T(8,128)(2,1)S(1)}) custom-call(bf16[2,1,64,256]{3,2,1,0:T(8,128)(2,1)} %bitcast.19, bf16[2,1,64,256]{3,2,1,0:T(8,128)(2,1)} %bitcast.17, ...), custom_call_target="tpu_custom_call" | custom-call | tf_op jit(solution)/shard_map/prepare/pallas_call | solution.py:319
  5.9 0.4 collective-permute-done.1.refs_3_
  6.3 1.9 %collective-permute-done.refs_1_ = bf16[2,1,64,256]{3,2,1,0:T(8,128)(2,1)S(1)} collective-permute-done((bf16[2,1,64,256]{3,2,1,0:T(8,128)(2,1)}, bf16[2,1,64,256]{3,2,1,0:T(8,128)(2,1)S(1)}, u32[]{:S(2)}, u32[]{:S(2)}) %collective-permute-start) | collective-permute-done | bytes 65568 | tf_op jit(solution)/shard_map/ppermute | solution.py:27
  8.1 0.0 copy-start
  8.1 0.1 first_block.1
  8.3 5.0 %collective-permute-start.2 = (bf16[2,256,128]{2,1,0:T(8,128)(2,1)S(1)}, bf16[2,256,128]{2,1,0:T(8,128)(2,1)S(1)}, u32[]{:S(2)}, u32[]{:S(2)}) collective-permute-start(bf16[2,256,128]{2,1,0:T(8,128)(2,1)S(1)} %get-tuple-element.25.refs_0_), channel_id=1, source_target_pairs={{8,0},{16,8},{24,16},{0,24},{9,1},{17,9},{25,17},{1,25},{10,2},{18... | collective-permute-start | bytes 393224 | tf_op jit(solution)/shard_map/ppermute | solution.py:348
  13.3 0.0 copy-done
  13.3 1.0 %collective-permute-start.3 = (bf16[2,1,64,256]{3,2,1,0:T(8,128)(2,1)S(1)}, bf16[2,1,64,256]{3,2,1,0:T(8,128)(2,1)S(1)}, u32[]{:S(2)}, u32[]{:S(2)}) collective-permute-start(bf16[2,1,64,256]{3,2,1,0:T(8,128)(2,1)S(1)} %bitcast.21), channel_id=1, source_target_pairs={{1,0},{0,1},{3,2},{2,3},{5,4},{4,5},{7,6},{6,7},{9,8},{8,9},{11,10... | collective-permute-start | bytes 196616 | tf_op jit(solution)/shard_map/ppermute | solution.py:27
  14.2 3.3 %collective-permute-done.3.refs_2_ = bf16[2,1,64,256]{3,2,1,0:T(8,128)(2,1)S(1)} collective-permute-done((bf16[2,1,64,256]{3,2,1,0:T(8,128)(2,1)S(1)}, bf16[2,1,64,256]{3,2,1,0:T(8,128)(2,1)S(1)}, u32[]{:S(2)}, u32[]{:S(2)}) %collective-permute-start.3) | collective-permute-done | bytes 65568 | tf_op jit(solution)/shard_map/ppermute | solution.py:27
  17.5 0.1 pack.1
  17.7 0.0 collective-permute-done.2.grad_ref.refs_1_
  17.7 0.7 %collective-permute-start.4 = (bf16[2,256,128]{2,1,0:T(8,128)(2,1)S(1)}, bf16[2,256,128]{2,1,0:T(8,128)(2,1)S(1)}, u32[]{:S(2)}, u32[]{:S(2)}) collective-permute-start(bf16[2,256,128]{2,1,0:T(8,128)(2,1)S(1)} %block.3.refs_1_), channel_id=1, source_target_pairs={{0,0},{8,16},{16,8},{24,24},{1,1},{9,17},{17,9},{25,25},{2,2},{10,... | collective-permute-start | bytes 393224 | tf_op jit(solution)/shard_map/ppermute | solution.py:348
  18.4 1.6 %collective-permute-start.8 = (bf16[2,320,128]{2,1,0:T(8,128)(2,1)S(1)}, bf16[2,320,128]{2,1,0:T(8,128)(2,1)S(1)}, u32[]{:S(2)}, u32[]{:S(2)}) collective-permute-start(bf16[2,320,128]{2,1,0:T(8,128)(2,1)S(1)} %get-tuple-element.30), channel_id=1, source_target_pairs={{4,0},{6,2},{0,4},{2,6},{5,1},{7,3},{1,5},{3,7},{12,8},{14,10},{8,... | collective-permute-start | bytes 491528 | tf_op jit(solution)/shard_map/ppermute | solution.py:360
  19.9 0.0 collective-permute-done.4.grad_ref.refs_2_
  19.9 6.9 %collective-permute-start.5 = (bf16[2,256,128]{2,1,0:T(8,128)(2,1)S(1)}, bf16[2,256,128]{2,1,0:T(8,128)(2,1)S(1)}, u32[]{:S(2)}, u32[]{:S(2)}) collective-permute-start(bf16[2,256,128]{2,1,0:T(8,128)(2,1)S(1)} %block.4.refs_2_), channel_id=1, source_target_pairs={{0,8},{8,0},{16,16},{24,24},{1,9},{9,1},{17,17},{25,25},{2,10},{10... | collective-permute-start | bytes 393224 | tf_op jit(solution)/shard_map/ppermute | solution.py:348
  26.9 0.1 collective-permute-start.9
  26.9 1.6 %collective-permute-start.10 = (bf16[2,320,128]{2,1,0:T(8,128)(2,1)S(1)}, bf16[2,320,128]{2,1,0:T(8,128)(2,1)S(1)}, u32[]{:S(2)}, u32[]{:S(2)}) collective-permute-start(bf16[2,320,128]{2,1,0:T(8,128)(2,1)S(1)} %get-tuple-element.32), channel_id=1, source_target_pairs={{2,0},{0,2},{6,4},{4,6},{3,1},{1,3},{7,5},{5,7},{10,8},{8,10},{14,... | collective-permute-start | bytes 491528 | tf_op jit(solution)/shard_map/ppermute | solution.py:360
  28.5 1.3 %collective-permute-done.5.grad_ref.refs_3_ = bf16[2,256,128]{2,1,0:T(8,128)(2,1)S(1)} collective-permute-done((bf16[2,256,128]{2,1,0:T(8,128)(2,1)S(1)}, bf16[2,256,128]{2,1,0:T(8,128)(2,1)S(1)}, u32[]{:S(2)}, u32[]{:S(2)}) %collective-permute-start.5) | collective-permute-done | bytes 131104 | tf_op jit(solution)/shard_map/ppermute | solution.py:348
  29.8 0.1 collective-permute-start.11
  29.9 1.6 %collective-permute-start.7 = (bf16[2,256,128]{2,1,0:T(8,128)(2,1)S(1)}, bf16[2,256,128]{2,1,0:T(8,128)(2,1)S(1)}, u32[]{:S(2)}, u32[]{:S(2)}) collective-permute-start(bf16[2,256,128]{2,1,0:T(8,128)(2,1)S(1)} %choose.1.refs_0_), channel_id=1, source_target_pairs={{6,0},{4,2},{2,4},{0,6},{7,1},{5,3},{3,5},{1,7},{14,8},{12,10},{10... | collective-permute-start | bytes 393224 | tf_op jit(solution)/shard_map/ppermute | solution.py:27
  31.5 0.0 collective-permute-done.8.refs_2_
  31.5 0.5 %collective-permute-start.6 = (bf16[2,256,128]{2,1,0:T(8,128)(2,1)S(1)}, bf16[2,256,128]{2,1,0:T(8,128)(2,1)S(1)}, u32[]{:S(2)}, u32[]{:S(2)}) collective-permute-start(bf16[2,256,128]{2,1,0:T(8,128)(2,1)S(1)} %choose.1.refs_0_), channel_id=1, source_target_pairs={{4,0},{6,2},{0,4},{2,6},{5,1},{7,3},{1,5},{3,7},{12,8},{14,10},{8,... | collective-permute-start | bytes 393224 | tf_op jit(solution)/shard_map/ppermute | solution.py:27
  32.0 1.3 %collective-permute-done.9.refs_3_ = bf16[2,320,128]{2,1,0:T(8,128)(2,1)S(1)} collective-permute-done((bf16[2,320,128]{2,1,0:T(8,128)(2,1)S(1)}, bf16[2,320,128]{2,1,0:T(8,128)(2,1)S(1)}, u32[]{:S(2)}, u32[]{:S(2)}) %collective-permute-start.9) | collective-permute-done | bytes 163872 | tf_op jit(solution)/shard_map/ppermute | solution.py:360
  33.4 0.0 collective-permute-done.10.refs_1_.refs_3_
  33.4 0.4 unfold.1
  33.8 1.4 %block.5.refs_3_ = bf16[2,256,128]{2,1,0:T(8,128)(2,1)S(1)} custom-call(bf16[2,256,128]{2,1,0:T(8,128)(2,1)S(1)} %collective-permute-done.5.grad_ref.refs_3_, bf16[2,256,128]{2,1,0:T(8,128)(2,1)S(1)} %get-tuple-element.26.refs_0_.pre_ref, bf16[27,256,256]{2,1,0:T(8,128)(2,1)S(1)} %get-tuple-element.23.refs_4_.conv_ref, ...), custom_call_target="tpu_custom_call" | custom-call | tf_op jit(solution)/shard_map/block/pallas_call | solution.py:375
  35.1 0.8 %own_grads.1 = bf16[2,1,64,256]{3,2,1,0:T(8,128)(2,1)} custom-call(bf16[2,256,128]{2,1,0:T(8,128)(2,1)S(1)} %get-tuple-element.25.refs_0_, bf16[2,256,128]{2,1,0:T(8,128)(2,1)S(1)} %block.3.refs_1_, bf16[2,256,128]{2,1,0:T(8,128)(2,1)S(1)} %block.4.refs_2_, bf16[2,256,128]{2,1,0:T(8,128)(2,1)S(1)} %block.5.refs_3_), custom_call_target="tpu_custom_call" | custom-call | tf_op jit(solution)/shard_map/own_grads/pallas_call | solution.py:428
  35.9 0.0 collective-permute-done.11.refs_1_
  35.9 0.9 %near_weight_grads.1 = (f32[1728,256]{1,0:T(8,128)S(1)}, f32[64,256]{1,0:T(8,128)S(1)}) custom-call(bf16[2,256,128]{2,1,0:T(8,128)(2,1)S(1)} %choose.1.refs_0_, bf16[2,256,128]{2,1,0:T(8,128)(2,1)S(1)} %collective-permute-done.11.refs_1_, bf16[2,320,128]{2,1,0:T(8,128)(2,1)S(1)} %get-tuple-element.28.refs_0_.refs_2_, ...), custom_call_target="tpu_custom_call" | custom-call | tf_op jit(solution)/shard_map/near_weight_grads/pallas_call | solution.py:402
  36.8 0.0 collective-permute-done.7.refs_1_
  36.8 2.2 %collective-permute-done.6.refs_0_ = bf16[2,256,128]{2,1,0:T(8,128)(2,1)S(1)} collective-permute-done((bf16[2,256,128]{2,1,0:T(8,128)(2,1)S(1)}, bf16[2,256,128]{2,1,0:T(8,128)(2,1)S(1)}, u32[]{:S(2)}, u32[]{:S(2)}) %collective-permute-start.6) | collective-permute-done | bytes 131104 | tf_op jit(solution)/shard_map/ppermute | solution.py:27
  39.0 2.4 %far_weight_grads.1 = (f32[1728,256]{1,0:T(8,128)}, f32[64,256]{1,0:T(8,128)}) custom-call(bf16[2,256,128]{2,1,0:T(8,128)(2,1)S(1)} %collective-permute-done.6.refs_0_, bf16[2,256,128]{2,1,0:T(8,128)(2,1)S(1)} %collective-permute-done.7.refs_1_, bf16[2,320,128]{2,1,0:T(8,128)(2,1)S(1)} %collective-permute-done.8.refs_2_, ...), custom_call_target="tpu_custom_call" | custom-call | tf_op jit(solution)/shard_map/far_weight_grads/pallas_call | solution.py:414
  (3 shorter events, 0.0 us)
Async XLA Ops:
  0.6 5.6 %collective-permute-start.1 = (bf16[2,1,64,256]{3,2,1,0:T(8,128)(2,1)}, bf16[2,1,64,256]{3,2,1,0:T(8,128)(2,1)S(1)}, u32[]{:S(2)}, u32[]{:S(2)}) collective-permute-start(bf16[2,1,64,256]{3,2,1,0:T(8,128)(2,1)} %bitcast.16), channel_id=1, source_target_pairs={{1,0},{0,1},{3,2},{2,3},{5,4},{4,5},{7,6},{6,7},{9,8},{8,9},{11,10... | collective-permute-start | bytes 196616 | tf_op jit(solution)/shard_map/ppermute | solution.py:27
  3.7 4.5 %collective-permute-start = (bf16[2,1,64,256]{3,2,1,0:T(8,128)(2,1)}, bf16[2,1,64,256]{3,2,1,0:T(8,128)(2,1)S(1)}, u32[]{:S(2)}, u32[]{:S(2)}) collective-permute-start(bf16[2,1,64,256]{3,2,1,0:T(8,128)(2,1)} %bitcast.18), channel_id=1, source_target_pairs={{1,0},{0,1},{3,2},{2,3},{5,4},{4,5},{7,6},{6,7},{9,8},{8,9},{11,10... | collective-permute-start | bytes 196616 | tf_op jit(solution)/shard_map/ppermute | solution.py:27
  8.1 5.1 %copy-start = (bf16[1,2,1,1,8,8,256]{6,5,4,3,2,1,0:T(8,128)(2,1)S(1)}, bf16[1,2,1,1,8,8,256]{6,5,4,3,2,1,0:T(8,128)(2,1)}, u32[]{:S(2)}) copy-start(bf16[1,2,1,1,8,8,256]{6,5,4,3,2,1,0:T(8,128)(2,1)} %param.5) | copy-start | bytes 196612
  8.3 9.4 %collective-permute-start.2 = (bf16[2,256,128]{2,1,0:T(8,128)(2,1)S(1)}, bf16[2,256,128]{2,1,0:T(8,128)(2,1)S(1)}, u32[]{:S(2)}, u32[]{:S(2)}) collective-permute-start(bf16[2,256,128]{2,1,0:T(8,128)(2,1)S(1)} %get-tuple-element.25.refs_0_), channel_id=1, source_target_pairs={{8,0},{16,8},{24,16},{0,24},{9,1},{17,9},{25,17},{1,25},{10,2},{18... | collective-permute-start | bytes 393224 | tf_op jit(solution)/shard_map/ppermute | solution.py:348
  13.3 4.3 %collective-permute-start.3 = (bf16[2,1,64,256]{3,2,1,0:T(8,128)(2,1)S(1)}, bf16[2,1,64,256]{3,2,1,0:T(8,128)(2,1)S(1)}, u32[]{:S(2)}, u32[]{:S(2)}) collective-permute-start(bf16[2,1,64,256]{3,2,1,0:T(8,128)(2,1)S(1)} %bitcast.21), channel_id=1, source_target_pairs={{1,0},{0,1},{3,2},{2,3},{5,4},{4,5},{7,6},{6,7},{9,8},{8,9},{11,10... | collective-permute-start | bytes 196616 | tf_op jit(solution)/shard_map/ppermute | solution.py:27
  17.7 2.2 %collective-permute-start.4 = (bf16[2,256,128]{2,1,0:T(8,128)(2,1)S(1)}, bf16[2,256,128]{2,1,0:T(8,128)(2,1)S(1)}, u32[]{:S(2)}, u32[]{:S(2)}) collective-permute-start(bf16[2,256,128]{2,1,0:T(8,128)(2,1)S(1)} %block.3.refs_1_), channel_id=1, source_target_pairs={{0,0},{8,16},{16,8},{24,24},{1,1},{9,17},{17,9},{25,25},{2,2},{10,... | collective-permute-start | bytes 393224 | tf_op jit(solution)/shard_map/ppermute | solution.py:348
  18.4 13.1 %collective-permute-start.8 = (bf16[2,320,128]{2,1,0:T(8,128)(2,1)S(1)}, bf16[2,320,128]{2,1,0:T(8,128)(2,1)S(1)}, u32[]{:S(2)}, u32[]{:S(2)}) collective-permute-start(bf16[2,320,128]{2,1,0:T(8,128)(2,1)S(1)} %get-tuple-element.30), channel_id=1, source_target_pairs={{4,0},{6,2},{0,4},{2,6},{5,1},{7,3},{1,5},{3,7},{12,8},{14,10},{8,... | collective-permute-start | bytes 491528 | tf_op jit(solution)/shard_map/ppermute | solution.py:360
  19.9 9.8 %collective-permute-start.5 = (bf16[2,256,128]{2,1,0:T(8,128)(2,1)S(1)}, bf16[2,256,128]{2,1,0:T(8,128)(2,1)S(1)}, u32[]{:S(2)}, u32[]{:S(2)}) collective-permute-start(bf16[2,256,128]{2,1,0:T(8,128)(2,1)S(1)} %block.4.refs_2_), channel_id=1, source_target_pairs={{0,8},{8,0},{16,16},{24,24},{1,9},{9,1},{17,17},{25,25},{2,10},{10... | collective-permute-start | bytes 393224 | tf_op jit(solution)/shard_map/ppermute | solution.py:348
  26.9 6.5 %collective-permute-start.9 = (bf16[2,320,128]{2,1,0:T(8,128)(2,1)S(1)}, bf16[2,320,128]{2,1,0:T(8,128)(2,1)S(1)}, u32[]{:S(2)}, u32[]{:S(2)}) collective-permute-start(bf16[2,320,128]{2,1,0:T(8,128)(2,1)S(1)} %get-tuple-element.31), channel_id=1, source_target_pairs={{6,0},{4,2},{2,4},{0,6},{7,1},{5,3},{3,5},{1,7},{14,8},{12,10},{10... | collective-permute-start | bytes 491528 | tf_op jit(solution)/shard_map/ppermute | solution.py:360
  26.9 6.4 %collective-permute-start.10 = (bf16[2,320,128]{2,1,0:T(8,128)(2,1)S(1)}, bf16[2,320,128]{2,1,0:T(8,128)(2,1)S(1)}, u32[]{:S(2)}, u32[]{:S(2)}) collective-permute-start(bf16[2,320,128]{2,1,0:T(8,128)(2,1)S(1)} %get-tuple-element.32), channel_id=1, source_target_pairs={{2,0},{0,2},{6,4},{4,6},{3,1},{1,3},{7,5},{5,7},{10,8},{8,10},{14,... | collective-permute-start | bytes 491528 | tf_op jit(solution)/shard_map/ppermute | solution.py:360
  29.8 6.1 %collective-permute-start.11 = (bf16[2,256,128]{2,1,0:T(8,128)(2,1)S(1)}, bf16[2,256,128]{2,1,0:T(8,128)(2,1)S(1)}, u32[]{:S(2)}, u32[]{:S(2)}) collective-permute-start(bf16[2,256,128]{2,1,0:T(8,128)(2,1)S(1)} %choose.1.refs_0_), channel_id=1, source_target_pairs={{2,0},{0,2},{6,4},{4,6},{3,1},{1,3},{7,5},{5,7},{10,8},{8,10},{14,... | collective-permute-start | bytes 393224 | tf_op jit(solution)/shard_map/ppermute | solution.py:27
  29.9 6.9 %collective-permute-start.7 = (bf16[2,256,128]{2,1,0:T(8,128)(2,1)S(1)}, bf16[2,256,128]{2,1,0:T(8,128)(2,1)S(1)}, u32[]{:S(2)}, u32[]{:S(2)}) collective-permute-start(bf16[2,256,128]{2,1,0:T(8,128)(2,1)S(1)} %choose.1.refs_0_), channel_id=1, source_target_pairs={{6,0},{4,2},{2,4},{0,6},{7,1},{5,3},{3,5},{1,7},{14,8},{12,10},{10... | collective-permute-start | bytes 393224 | tf_op jit(solution)/shard_map/ppermute | solution.py:27
  31.5 7.5 %collective-permute-start.6 = (bf16[2,256,128]{2,1,0:T(8,128)(2,1)S(1)}, bf16[2,256,128]{2,1,0:T(8,128)(2,1)S(1)}, u32[]{:S(2)}, u32[]{:S(2)}) collective-permute-start(bf16[2,256,128]{2,1,0:T(8,128)(2,1)S(1)} %choose.1.refs_0_), channel_id=1, source_target_pairs={{4,0},{6,2},{0,4},{2,6},{5,1},{7,3},{1,5},{3,7},{12,8},{14,10},{8,... | collective-permute-start | bytes 393224 | tf_op jit(solution)/shard_map/ppermute | solution.py:27

commit v2 on v0

--- a/solution.py
+++ b/solution.py
@@ -143,34 +143,54 @@
             out_ref[z] = result[z]
 
 
-def pack_kernel(others, *refs):
-    pre_ref, acts_ref, acts_rows = refs[0], refs[1], refs[2 : 2 + others]
-    parcel_refs, scratch = refs[2 + others : -1], refs[-1]
-    here = lax.axis_index("space")
+def pack_kernel(pre_ref, acts_ref, *refs):
+    parcel_refs, scratch = refs[:-1], refs[-1]
     place = lax.axis_index("dp")
     count = len(parcel_refs)
-    planes, channels = pre_ref.shape[:2]
+    planes, channels, lanes = pre_ref.shape
+    depth_dev = acts_ref.shape[0]
     shard = channels // count
-    padded = parcel_refs[0].shape[1] - channels
-    placed_planes(here, acts_ref, acts_rows, scratch)
-    for distance in range(count):
+    padded = (parcel_refs[0].shape[0] - planes * channels) // depth_dev
+    scratch[...] = acts_ref[...].astype(jnp.float32)
+    for distance, parcel_ref in enumerate(parcel_refs):
         target = peer(place, distance, count, back=True)
         for z in range(planes):
-            parcel_refs[distance][z, :channels] = pre_ref[z]
-            rows = scratch[z, pl.ds(pl.multiple_of(target * shard, shard), shard)]
-            parcel_refs[distance][z, channels : channels + shard] = rows.astype(jnp.bfloat16)
+            parcel_ref[z * channels : (z + 1) * channels] = pre_ref[z]
+        for depth in range(depth_dev):
+            rows = scratch[depth, pl.ds(pl.multiple_of(target * shard, shard), shard)]
             if padded > shard:
-                parcel_refs[distance][z, channels + shard :] = jnp.zeros(
-                    (padded - shard, rows.shape[1]), jnp.bfloat16
-                )
-
-
-def unfold_kernel(height, width, channels, shard, near, *refs):
-    parcel_refs, near_ref, far_ref = refs[:-2], refs[-2], refs[-1]
+                blank = jnp.zeros((padded - shard, lanes), jnp.float32)
+                rows = jnp.concatenate([rows, blank], axis=0)
+            start = planes * channels + depth * padded
+            parcel_ref[start : start + padded] = rows.astype(jnp.bfloat16)
+
+
+def collect_kernel(*refs):
+    parcel_refs, mine_ref = refs[:-1], refs[-1]
+    depth_dev, rows = mine_ref.shape[:2]
+    padded = rows // len(parcel_refs)
     for place, parcel_ref in enumerate(parcel_refs):
+        for depth in range(depth_dev):
+            start = parcel_ref.shape[0] - (depth_dev - depth) * padded
+            mine_ref[depth, place * padded : (place + 1) * padded] = parcel_ref[
+                start : start + padded
+            ]
+
+
+def unfold_kernel(height, width, others, shard, near, *refs):
+    slab_refs, near_ref, far_ref, scratch = refs[: others + 1], *refs[others + 2 :]
+    here = lax.axis_index("space")
+    count = lax.axis_size("dp")
+    depth_dev, rows, lanes = slab_refs[0].shape
+    padded = rows // count
+    for distance, slab_ref in enumerate(slab_refs):
+        for depth in range(depth_dev):
+            z = peer(here, distance, others + 1) * depth_dev + depth
+            scratch[z] = slab_ref[depth].astype(jnp.float32)
+    depth_all = scratch.shape[0]
+    for place in range(count):
         planes = [
-            parcel_ref[z, channels:].astype(jnp.float32)[:shard]
-            for z in range(parcel_ref.shape[0])
+            scratch[z, place * padded : (place + 1) * padded][:shard] for z in range(depth_all)
         ]
         moved = [
             [shifted(plane, row_off, col_off, height, width) for row_off, col_off in PLANE_TAPS]
@@ -178,15 +198,15 @@
         ]
         blank = jnp.zeros_like(planes[0])
         columns = []
-        for z in range(len(planes)):
+        for z in range(depth_all):
             taps = []
             for depth_off in SIDE:
-                inside = 0 <= z + depth_off < len(planes)
+                inside = 0 <= z + depth_off < depth_all
                 taps.extend(moved[z + depth_off] if inside else [blank] * len(PLANE_TAPS))
             columns.append(jnp.concatenate(taps, axis=0).astype(jnp.bfloat16))
-        lanes = planes[0].shape[1] * len(planes)
+        span = lanes * depth_all
         target, start = (near_ref, place) if place < near else (far_ref, place - near)
-        target[:, start * lanes : (start + 1) * lanes] = jnp.concatenate(columns, axis=1)
+        target[:, start * span : (start + 1) * span] = jnp.concatenate(columns, axis=1)
 
 
 def choose_kernel(count, *refs):
@@ -205,14 +225,21 @@
     for place, (grad_ref, parcel_ref) in enumerate(zip(grad_refs, parcel_refs)):
         planes = grad_ref.shape[0]
         grad = jnp.concatenate([grad_ref[z] for z in range(planes)], axis=1)
-        pre = jnp.concatenate([parcel_ref[z, :channels] for z in range(planes)], axis=1)
+        pre = jnp.concatenate(
+            [parcel_ref[z * channels : (z + 1) * channels] for z in range(planes)], axis=1
+        )
         hidden_grad = jnp.dot(proj_ref[...], grad, preferred_element_type=jnp.float32)
         lanes = grad.shape[1]
         masked_ref[:, place * lanes : (place + 1) * lanes] = jnp.where(
             pre.astype(jnp.float32) > 0, hidden_grad, 0.0
         ).astype(jnp.bfloat16)
-        rows = pl.ds(pl.multiple_of(here * shard, shard), shard)
-        mine = jnp.concatenate([parcel_ref[z, rows] for z in range(planes)], axis=1)
+        mine = jnp.concatenate(
+            [
+                parcel_ref[pl.ds(pl.multiple_of(z * channels + here * shard, shard), shard)]
+                for z in range(planes)
+            ],
+            axis=1,
+        )
         hidden = jnp.maximum(mine.astype(jnp.float32), 0.0).astype(jnp.bfloat16)
         term = lax.dot_general(
             hidden, grad, CONTRACT_LANES, preferred_element_type=jnp.float32
@@ -302,11 +329,10 @@
     volume = jax.ShapeDtypeStruct((planes, channels, lanes), bfloat)
     slab = jax.ShapeDtypeStruct((depth_dev, channels, lanes), bfloat)
     padded = -(-shard // 16) * 16
-    parcel = jax.ShapeDtypeStruct((planes, channels + padded, lanes), bfloat)
+    parcel = jax.ShapeDtypeStruct((planes * channels + depth_dev * padded, lanes), bfloat)
 
     seed_rows = neighbours(seeds, "space")[1:]
     pre_rows = neighbours(pre_acts, "space")[1:]
-    acts_rows = neighbours(acts, "space")[1:]
 
     seed_own, pre_own, acts_own, conv_weight, proj_weight = pl.pallas_call(
         prepare_kernel,
@@ -335,21 +361,20 @@
 
     results = [result]
     received = []
+    ring = [((i + 1) % section_count, i) for i in range(section_count)]
     parcels = None
     for step in range(1, section_count):
-        senders = section_count + 1 - step
-        ring = [((i + 1) % senders, i) for i in range(senders)]
         received.append(lax.ppermute(results[-1], "section", ring))
         if parcels is None:
             sent = pl.pallas_call(
-                functools.partial(pack_kernel, others),
+                pack_kernel,
                 out_shape=(parcel,) * crop_count,
-                in_specs=whole(2 + others),
+                in_specs=whole(2),
                 out_specs=tuple(whole(crop_count)),
-                scratch_shapes=[pltpu.VMEM(volume.shape, jnp.float32)],
+                scratch_shapes=[pltpu.VMEM(slab.shape, jnp.float32)],
                 compiler_params=params(),
                 name="pack",
-            )(pre_all, acts_own, *acts_rows)
+            )(pre_all, acts_own)
             parcels = [sent[0]] + [
                 lax.ppermute(
                     sent[distance],
@@ -358,6 +383,15 @@
                 )
                 for distance in range(1, crop_count)
             ]
+            acts_mine = pl.pallas_call(
+                collect_kernel,
+                out_shape=jax.ShapeDtypeStruct((depth_dev, crop_count * padded, lanes), bfloat),
+                in_specs=whole(crop_count),
+                out_specs=whole()[0],
+                compiler_params=params(),
+                name="collect",
+            )(*parcels)
+        earlier = parcels[0] if step == 1 else acts_mine
         step_call = pl.pallas_call(
             functools.partial(step_kernel, step, height, width),
             out_shape=volume,
@@ -366,7 +400,7 @@
             compiler_params=params(),
             name="block",
         )
-        results.append(step_call(received[-1], pre_all, conv_weight, proj_weight, parcels[0]))
+        results.append(step_call(received[-1], pre_all, conv_weight, proj_weight, earlier))
     grad_own = pl.pallas_call(
         functools.partial(choose_kernel, section_count),
         out_shape=volume,
@@ -380,16 +414,17 @@
     near = crop_count // 2
     span = planes * lanes
     near_unfolded, far_unfolded = pl.pallas_call(
-        functools.partial(unfold_kernel, height, width, channels, shard, near),
+        functools.partial(unfold_kernel, height, width, others, shard, near),
         out_shape=(
             jax.ShapeDtypeStruct((taps * shard, near * span), bfloat),
             jax.ShapeDtypeStruct((taps * shard, (crop_count - near) * span), bfloat),
         ),
-        in_specs=whole(crop_count),
+        in_specs=whole(space_count) + [pl.BlockSpec(memory_space=pl.ANY)],
         out_specs=tuple(whole(2)),
+        scratch_shapes=[pltpu.VMEM((planes, crop_count * padded, lanes), jnp.float32)],
         compiler_params=params(),
         name="unfold",
-    )(*parcels)
+    )(*neighbours(acts_mine, "space"), results[-1])
 
     conv_shape = jax.ShapeDtypeStruct((taps * shard, channels), jnp.float32)
     proj_shape = jax.ShapeDtypeStruct((shard, channels), jnp.float32)

time: 42.8 us -> 40.7 us (0.951)
  waiting for transfers between devices: 13.9 us -> 9.89 us
  starting transfers between devices: 19.8 us -> 21.7 us
    ppermute x6, waiting for transfers between devices: 8.34 us -> 4.36 us  [neighbours(): blocks.append(lax.ppermute(block, axis, pairs))]
    ppermute x3, starting transfers between devices: 10.2 us -> 13.5 us  [shards(): received.append(lax.ppermute(results[-1], 'section', ring))]
    ppermute x3, waiting for transfers between devices: 5.25 us -> 3.16 us  [shards(): received.append(lax.ppermute(results[-1], 'section', ring))]
    ppermute x3, waiting for transfers between devices: 0.29 us -> 2.37 us  [shards(): lax.ppermute(sent[distance], 'dp', [(peer(i, distance, crop_count), i) fo...]
    ppermute x3, starting transfers between devices: 3.22 us -> 1.93 us  [shards(): lax.ppermute(sent[distance], 'dp', [(peer(i, distance, crop_count), i) fo...]
    pallas_call x5 -> x6, Pallas kernels: 1.89 us -> 1.85 us  [the longest x3 1.37 us: shards(): step_call(received[-1], pre_all, conv_weight, proj_weight, earlier)]
  transfers between devices with their start and end apart: 12 -> 12, of which waited for: 7 -> 9; matrix products, arithmetic and copies ran while one was open for 0% -> 0% of each run, Pallas kernels for 13% -> 14%
where the time goes in v2:
time: 40.7 us; the launch traced here: 40.5 us
  starting transfers between devices  21.7 us (53%)
  waiting for transfers between devices  9.89 us (24%)
  Pallas kernels  8.21 us (20%)
  between operations  0.71 us (2%)
    ppermute x3, starting transfers between devices, shards(): received.append(lax.ppermute(results[-1], 'section', ring))  13.5 us
    ppermute x6, starting transfers between devices, neighbours(): blocks.append(lax.ppermute(block, axis, pairs))  6.29 us
    ppermute x6, waiting for transfers between devices, neighbours(): blocks.append(lax.ppermute(block, axis, pairs))  4.36 us
    ppermute x3, waiting for transfers between devices, shards(): received.append(lax.ppermute(results[-1], 'section', ring))  3.16 us
    pallas_call x1, Pallas kernels, shards(): pl.pallas_call(functools.partial(far_kernel, far, channels, shard, scale_...  2.45 us
    ppermute x3, waiting for transfers between devices, shards(): lax.ppermute(sent[distance], 'dp', [(peer(i, distance, crop_count), i) fo...  2.37 us
    pallas_call x1, Pallas kernels, shards(): pl.pallas_call(prepare_kernel, out_shape=(slab, slab, slab, jax.ShapeDtyp...  2.16 us
    ppermute x3, starting transfers between devices, shards(): lax.ppermute(sent[distance], 'dp', [(peer(i, distance, crop_count), i) fo...  1.93 us
  transfers between devices with their start and end apart: 12, of which 9 were waited for; matrix products, arithmetic and copies ran while one was open for 0% of the time, Pallas kernels for 14%

profile of v2, /device:TPU:0, one launch (start us, length us, event | category | flops | bytes accessed | tf_op | source)
XLA Modules:
  0.0 40.5 jit_solution(9913263336785594145)
XLA Ops:
  0.6 3.0 %collective-permute-start.1 = (bf16[2,1,64,256]{3,2,1,0:T(8,128)(2,1)}, bf16[2,1,64,256]{3,2,1,0:T(8,128)(2,1)S(1)}, u32[]{:S(2)}, u32[]{:S(2)}) collective-permute-start(bf16[2,1,64,256]{3,2,1,0:T(8,128)(2,1)} %bitcast.17), channel_id=1, source_target_pairs={{1,0},{0,1},{3,2},{2,3},{5,4},{4,5},{7,6},{6,7},{9,8},{8,9},{11,10... | collective-permute-start | bytes 196616 | tf_op jit(solution)/shard_map/ppermute | solution.py:27
  3.7 0.1 collective-permute-start
  3.7 2.2 %prepare.1 = (bf16[1,256,128]{2,1,0:T(8,128)(2,1)S(1)}, bf16[1,256,128]{2,1,0:T(8,128)(2,1)S(1)}, bf16[1,256,128]{2,1,0:T(8,128)(2,1)S(1)}, bf16[27,256,256]{2,1,0:T(8,128)(2,1)S(1)}, bf16[256,256]{1,0:T(8,128)(2,1)S(1)}) custom-call(bf16[2,1,64,256]{3,2,1,0:T(8,128)(2,1)} %bitcast.20, bf16[2,1,64,256]{3,2,1,0:T(8,128)(2,1)} %bitcast.18, ...), custom_call_target="tpu_custom_call" | custom-call | tf_op jit(solution)/shard_map/prepare/pallas_call | solution.py:337
  5.9 0.4 collective-permute-done.1.refs_3_
  6.3 1.9 %collective-permute-done.refs_1_ = bf16[2,1,64,256]{3,2,1,0:T(8,128)(2,1)S(1)} collective-permute-done((bf16[2,1,64,256]{3,2,1,0:T(8,128)(2,1)}, bf16[2,1,64,256]{3,2,1,0:T(8,128)(2,1)S(1)}, u32[]{:S(2)}, u32[]{:S(2)}) %collective-permute-start) | collective-permute-done | bytes 65568 | tf_op jit(solution)/shard_map/ppermute | solution.py:27
  8.1 0.1 first_block.1
  8.2 5.0 %collective-permute-start.2 = (bf16[2,256,128]{2,1,0:T(8,128)(2,1)S(1)}, bf16[2,256,128]{2,1,0:T(8,128)(2,1)S(1)}, u32[]{:S(2)}, u32[]{:S(2)}) collective-permute-start(bf16[2,256,128]{2,1,0:T(8,128)(2,1)S(1)} %get-tuple-element.25.refs_0_), channel_id=1, source_target_pairs={{8,0},{16,8},{24,16},{0,24},{9,1},{17,9},{25,17},{1,25},{10,2},{18... | collective-permute-start | bytes 393224 | tf_op jit(solution)/shard_map/ppermute | solution.py:367
  13.3 0.1 pack.1
  13.4 0.1 collective-permute-start.4
  13.4 1.6 %collective-permute-start.5 = (bf16[576,128]{1,0:T(8,128)(2,1)S(1)}, bf16[576,128]{1,0:T(8,128)(2,1)S(1)}, u32[]{:S(2)}, u32[]{:S(2)}) collective-permute-start(bf16[576,128]{1,0:T(8,128)(2,1)S(1)} %get-tuple-element.30), channel_id=1, source_target_pairs={{4,0},{6,2},{0,4},{2,6},{5,1},{7,3},{1,5},{3,7},{12,8},{14,10},{8,... | collective-permute-start | bytes 442376 | tf_op jit(solution)/shard_map/ppermute | solution.py:379
  15.0 0.3 collective-permute-start.6
  15.3 0.5 %collective-permute-done.2.grad_ref.refs_1_ = bf16[2,256,128]{2,1,0:T(8,128)(2,1)S(1)} collective-permute-done((bf16[2,256,128]{2,1,0:T(8,128)(2,1)S(1)}, bf16[2,256,128]{2,1,0:T(8,128)(2,1)S(1)}, u32[]{:S(2)}, u32[]{:S(2)}) %collective-permute-start.2) | collective-permute-done | bytes 131104 | tf_op jit(solution)/shard_map/ppermute | solution.py:367
  15.8 4.2 %collective-permute-start.3 = (bf16[2,256,128]{2,1,0:T(8,128)(2,1)S(1)}, bf16[2,256,128]{2,1,0:T(8,128)(2,1)S(1)}, u32[]{:S(2)}, u32[]{:S(2)}) collective-permute-start(bf16[2,256,128]{2,1,0:T(8,128)(2,1)S(1)} %block.3.refs_1_), channel_id=1, source_target_pairs={{8,0},{16,8},{24,16},{0,24},{9,1},{17,9},{25,17},{1,25},{10,2},{18... | collective-permute-start | bytes 393224 | tf_op jit(solution)/shard_map/ppermute | solution.py:367
  20.0 0.0 collective-permute-done.4.refs_1_.refs_3_
  20.0 0.1 collective-permute-done.5.refs_2_
  20.2 2.3 %collective-permute-done.6.refs_3_ = bf16[576,128]{1,0:T(8,128)(2,1)S(1)} collective-permute-done((bf16[576,128]{1,0:T(8,128)(2,1)S(1)}, bf16[576,128]{1,0:T(8,128)(2,1)S(1)}, u32[]{:S(2)}, u32[]{:S(2)}) %collective-permute-start.6) | collective-permute-done | bytes 147488 | tf_op jit(solution)/shard_map/ppermute | solution.py:379
  22.4 0.1 collective-permute-done.3.grad_ref.refs_2_
  22.6 4.2 %collective-permute-start.7 = (bf16[2,256,128]{2,1,0:T(8,128)(2,1)S(1)}, bf16[2,256,128]{2,1,0:T(8,128)(2,1)S(1)}, u32[]{:S(2)}, u32[]{:S(2)}) collective-permute-start(bf16[2,256,128]{2,1,0:T(8,128)(2,1)S(1)} %block.4.refs_2_), channel_id=1, source_target_pairs={{8,0},{16,8},{24,16},{0,24},{9,1},{17,9},{25,17},{1,25},{10,2},{18... | collective-permute-start | bytes 393224 | tf_op jit(solution)/shard_map/ppermute | solution.py:367
  26.8 2.5 %collective-permute-done.7.grad_ref.refs_3_ = bf16[2,256,128]{2,1,0:T(8,128)(2,1)S(1)} collective-permute-done((bf16[2,256,128]{2,1,0:T(8,128)(2,1)S(1)}, bf16[2,256,128]{2,1,0:T(8,128)(2,1)S(1)}, u32[]{:S(2)}, u32[]{:S(2)}) %collective-permute-start.7) | collective-permute-done | bytes 131104 | tf_op jit(solution)/shard_map/ppermute | solution.py:367
  29.3 0.1 collective-permute-start.11
  29.4 1.6 %collective-permute-start.9 = (bf16[2,256,128]{2,1,0:T(8,128)(2,1)S(1)}, bf16[2,256,128]{2,1,0:T(8,128)(2,1)S(1)}, u32[]{:S(2)}, u32[]{:S(2)}) collective-permute-start(bf16[2,256,128]{2,1,0:T(8,128)(2,1)S(1)} %choose.1.refs_0_), channel_id=1, source_target_pairs={{6,0},{4,2},{2,4},{0,6},{7,1},{5,3},{3,5},{1,7},{14,8},{12,10},{10... | collective-permute-start | bytes 393224 | tf_op jit(solution)/shard_map/ppermute | solution.py:27
  31.0 0.5 %collective-permute-start.8 = (bf16[2,256,128]{2,1,0:T(8,128)(2,1)S(1)}, bf16[2,256,128]{2,1,0:T(8,128)(2,1)S(1)}, u32[]{:S(2)}, u32[]{:S(2)}) collective-permute-start(bf16[2,256,128]{2,1,0:T(8,128)(2,1)S(1)} %choose.1.refs_0_), channel_id=1, source_target_pairs={{4,0},{6,2},{0,4},{2,6},{5,1},{7,3},{1,5},{3,7},{12,8},{14,10},{8,... | collective-permute-start | bytes 393224 | tf_op jit(solution)/shard_map/ppermute | solution.py:27
  31.6 1.0 %collective-permute-start.10 = (bf16[1,256,128]{2,1,0:T(8,128)(2,1)S(1)}, bf16[1,256,128]{2,1,0:T(8,128)(2,1)S(1)}, u32[]{:S(2)}, u32[]{:S(2)}) collective-permute-start(bf16[1,256,128]{2,1,0:T(8,128)(2,1)S(1)} %collect.1.refs_0_), channel_id=1, source_target_pairs={{1,0},{0,1},{3,2},{2,3},{5,4},{4,5},{7,6},{6,7},{9,8},{8,9},{11,10... | collective-permute-start | bytes 196616 | tf_op jit(solution)/shard_map/ppermute | solution.py:27
  32.5 1.4 %block.5.refs_3_.refs_2_ = bf16[2,256,128]{2,1,0:T(8,128)(2,1)S(1)} custom-call(bf16[2,256,128]{2,1,0:T(8,128)(2,1)S(1)} %collective-permute-done.7.grad_ref.refs_3_, bf16[2,256,128]{2,1,0:T(8,128)(2,1)S(1)} %get-tuple-element.26.pre_ref, bf16[27,256,256]{2,1,0:T(8,128)(2,1)S(1)} %get-tuple-element.23.refs_4_.conv_ref, ...), custom_call_target="tpu_custom_call" | custom-call | tf_op jit(solution)/shard_map/block/pallas_call | solution.py:403
  33.9 0.8 %own_grads.1 = bf16[2,1,64,256]{3,2,1,0:T(8,128)(2,1)} custom-call(bf16[2,256,128]{2,1,0:T(8,128)(2,1)S(1)} %get-tuple-element.25.refs_0_, bf16[2,256,128]{2,1,0:T(8,128)(2,1)S(1)} %block.3.refs_1_, bf16[2,256,128]{2,1,0:T(8,128)(2,1)S(1)} %block.4.refs_2_, bf16[2,256,128]{2,1,0:T(8,128)(2,1)S(1)} %block.5.refs_3_.refs_2_), custom_call_target="tpu_custom_call" | custom-call | tf_op jit(solution)/shard_map/own_grads/pallas_call | solution.py:457
  34.7 1.2 %collective-permute-done.10.refs_1_ = bf16[1,256,128]{2,1,0:T(8,128)(2,1)S(1)} collective-permute-done((bf16[1,256,128]{2,1,0:T(8,128)(2,1)S(1)}, bf16[1,256,128]{2,1,0:T(8,128)(2,1)S(1)}, u32[]{:S(2)}, u32[]{:S(2)}) %collective-permute-start.10) | collective-permute-done | bytes 65568 | tf_op jit(solution)/shard_map/ppermute | solution.py:27
  35.8 0.4 unfold.1
  36.2 0.0 collective-permute-done.11.refs_1_
  36.2 0.9 %near_weight_grads.1 = (f32[1728,256]{1,0:T(8,128)S(1)}, f32[64,256]{1,0:T(8,128)S(1)}) custom-call(bf16[2,256,128]{2,1,0:T(8,128)(2,1)S(1)} %choose.1.refs_0_, bf16[2,256,128]{2,1,0:T(8,128)(2,1)S(1)} %collective-permute-done.11.refs_1_, bf16[576,128]{1,0:T(8,128)(2,1)S(1)} %get-tuple-element.28.refs_0_.refs_2_, ...), custom_call_target="tpu_custom_call" | custom-call | tf_op jit(solution)/shard_map/near_weight_grads/pallas_call | solution.py:431
  37.1 0.0 collective-permute-done.9.refs_1_
  37.1 1.0 %collective-permute-done.8.refs_0_ = bf16[2,256,128]{2,1,0:T(8,128)(2,1)S(1)} collective-permute-done((bf16[2,256,128]{2,1,0:T(8,128)(2,1)S(1)}, bf16[2,256,128]{2,1,0:T(8,128)(2,1)S(1)}, u32[]{:S(2)}, u32[]{:S(2)}) %collective-permute-start.8) | collective-permute-done | bytes 131104 | tf_op jit(solution)/shard_map/ppermute | solution.py:27
  38.1 2.4 %far_weight_grads.1 = (f32[1728,256]{1,0:T(8,128)}, f32[64,256]{1,0:T(8,128)}) custom-call(bf16[2,256,128]{2,1,0:T(8,128)(2,1)S(1)} %collective-permute-done.8.refs_0_, bf16[2,256,128]{2,1,0:T(8,128)(2,1)S(1)} %collective-permute-done.9.refs_1_, bf16[576,128]{1,0:T(8,128)(2,1)S(1)} %collective-permute-done.5.refs_2_, ...), custom_call_target="tpu_custom_call" | custom-call | tf_op jit(solution)/shard_map/far_weight_grads/pallas_call | solution.py:443
  (4 shorter events, 0.0 us)
Async XLA Ops:
  0.6 5.6 %collective-permute-start.1 = (bf16[2,1,64,256]{3,2,1,0:T(8,128)(2,1)}, bf16[2,1,64,256]{3,2,1,0:T(8,128)(2,1)S(1)}, u32[]{:S(2)}, u32[]{:S(2)}) collective-permute-start(bf16[2,1,64,256]{3,2,1,0:T(8,128)(2,1)} %bitcast.17), channel_id=1, source_target_pairs={{1,0},{0,1},{3,2},{2,3},{5,4},{4,5},{7,6},{6,7},{9,8},{8,9},{11,10... | collective-permute-start | bytes 196616 | tf_op jit(solution)/shard_map/ppermute | solution.py:27
  3.7 4.5 %collective-permute-start = (bf16[2,1,64,256]{3,2,1,0:T(8,128)(2,1)}, bf16[2,1,64,256]{3,2,1,0:T(8,128)(2,1)S(1)}, u32[]{:S(2)}, u32[]{:S(2)}) collective-permute-start(bf16[2,1,64,256]{3,2,1,0:T(8,128)(2,1)} %bitcast.19), channel_id=1, source_target_pairs={{1,0},{0,1},{3,2},{2,3},{5,4},{4,5},{7,6},{6,7},{9,8},{8,9},{11,10... | collective-permute-start | bytes 196616 | tf_op jit(solution)/shard_map/ppermute | solution.py:27
  8.2 7.5 %collective-permute-start.2 = (bf16[2,256,128]{2,1,0:T(8,128)(2,1)S(1)}, bf16[2,256,128]{2,1,0:T(8,128)(2,1)S(1)}, u32[]{:S(2)}, u32[]{:S(2)}) collective-permute-start(bf16[2,256,128]{2,1,0:T(8,128)(2,1)S(1)} %get-tuple-element.25.refs_0_), channel_id=1, source_target_pairs={{8,0},{16,8},{24,16},{0,24},{9,1},{17,9},{25,17},{1,25},{10,2},{18... | collective-permute-start | bytes 393224 | tf_op jit(solution)/shard_map/ppermute | solution.py:367
  13.4 6.7 %collective-permute-start.4 = (bf16[576,128]{1,0:T(8,128)(2,1)S(1)}, bf16[576,128]{1,0:T(8,128)(2,1)S(1)}, u32[]{:S(2)}, u32[]{:S(2)}) collective-permute-start(bf16[576,128]{1,0:T(8,128)(2,1)S(1)} %get-tuple-element.29), channel_id=1, source_target_pairs={{2,0},{0,2},{6,4},{4,6},{3,1},{1,3},{7,5},{5,7},{10,8},{8,10},{14,... | collective-permute-start | bytes 442376 | tf_op jit(solution)/shard_map/ppermute | solution.py:379
  13.4 6.7 %collective-permute-start.5 = (bf16[576,128]{1,0:T(8,128)(2,1)S(1)}, bf16[576,128]{1,0:T(8,128)(2,1)S(1)}, u32[]{:S(2)}, u32[]{:S(2)}) collective-permute-start(bf16[576,128]{1,0:T(8,128)(2,1)S(1)} %get-tuple-element.30), channel_id=1, source_target_pairs={{4,0},{6,2},{0,4},{2,6},{5,1},{7,3},{1,5},{3,7},{12,8},{14,10},{8,... | collective-permute-start | bytes 442376 | tf_op jit(solution)/shard_map/ppermute | solution.py:379
  15.0 7.4 %collective-permute-start.6 = (bf16[576,128]{1,0:T(8,128)(2,1)S(1)}, bf16[576,128]{1,0:T(8,128)(2,1)S(1)}, u32[]{:S(2)}, u32[]{:S(2)}) collective-permute-start(bf16[576,128]{1,0:T(8,128)(2,1)S(1)} %get-tuple-element.31), channel_id=1, source_target_pairs={{6,0},{4,2},{2,4},{0,6},{7,1},{5,3},{3,5},{1,7},{14,8},{12,10},{10... | collective-permute-start | bytes 442376 | tf_op jit(solution)/shard_map/ppermute | solution.py:379
  15.8 6.8 %collective-permute-start.3 = (bf16[2,256,128]{2,1,0:T(8,128)(2,1)S(1)}, bf16[2,256,128]{2,1,0:T(8,128)(2,1)S(1)}, u32[]{:S(2)}, u32[]{:S(2)}) collective-permute-start(bf16[2,256,128]{2,1,0:T(8,128)(2,1)S(1)} %block.3.refs_1_), channel_id=1, source_target_pairs={{8,0},{16,8},{24,16},{0,24},{9,1},{17,9},{25,17},{1,25},{10,2},{18... | collective-permute-start | bytes 393224 | tf_op jit(solution)/shard_map/ppermute | solution.py:367
  22.6 6.8 %collective-permute-start.7 = (bf16[2,256,128]{2,1,0:T(8,128)(2,1)S(1)}, bf16[2,256,128]{2,1,0:T(8,128)(2,1)S(1)}, u32[]{:S(2)}, u32[]{:S(2)}) collective-permute-start(bf16[2,256,128]{2,1,0:T(8,128)(2,1)S(1)} %block.4.refs_2_), channel_id=1, source_target_pairs={{8,0},{16,8},{24,16},{0,24},{9,1},{17,9},{25,17},{1,25},{10,2},{18... | collective-permute-start | bytes 393224 | tf_op jit(solution)/shard_map/ppermute | solution.py:367
  29.3 6.9 %collective-permute-start.11 = (bf16[2,256,128]{2,1,0:T(8,128)(2,1)S(1)}, bf16[2,256,128]{2,1,0:T(8,128)(2,1)S(1)}, u32[]{:S(2)}, u32[]{:S(2)}) collective-permute-start(bf16[2,256,128]{2,1,0:T(8,128)(2,1)S(1)} %choose.1.refs_0_), channel_id=1, source_target_pairs={{2,0},{0,2},{6,4},{4,6},{3,1},{1,3},{7,5},{5,7},{10,8},{8,10},{14,... | collective-permute-start | bytes 393224 | tf_op jit(solution)/shard_map/ppermute | solution.py:27
  29.4 7.7 %collective-permute-start.9 = (bf16[2,256,128]{2,1,0:T(8,128)(2,1)S(1)}, bf16[2,256,128]{2,1,0:T(8,128)(2,1)S(1)}, u32[]{:S(2)}, u32[]{:S(2)}) collective-permute-start(bf16[2,256,128]{2,1,0:T(8,128)(2,1)S(1)} %choose.1.refs_0_), channel_id=1, source_target_pairs={{6,0},{4,2},{2,4},{0,6},{7,1},{5,3},{3,5},{1,7},{14,8},{12,10},{10... | collective-permute-start | bytes 393224 | tf_op jit(solution)/shard_map/ppermute | solution.py:27
  31.0 7.1 %collective-permute-start.8 = (bf16[2,256,128]{2,1,0:T(8,128)(2,1)S(1)}, bf16[2,256,128]{2,1,0:T(8,128)(2,1)S(1)}, u32[]{:S(2)}, u32[]{:S(2)}) collective-permute-start(bf16[2,256,128]{2,1,0:T(8,128)(2,1)S(1)} %choose.1.refs_0_), channel_id=1, source_target_pairs={{4,0},{6,2},{0,4},{2,6},{5,1},{7,3},{1,5},{3,7},{12,8},{14,10},{8,... | collective-permute-start | bytes 393224 | tf_op jit(solution)/shard_map/ppermute | solution.py:27
  31.6 4.3 %collective-permute-start.10 = (bf16[1,256,128]{2,1,0:T(8,128)(2,1)S(1)}, bf16[1,256,128]{2,1,0:T(8,128)(2,1)S(1)}, u32[]{:S(2)}, u32[]{:S(2)}) collective-permute-start(bf16[1,256,128]{2,1,0:T(8,128)(2,1)S(1)} %collect.1.refs_0_), channel_id=1, source_target_pairs={{1,0},{0,1},{3,2},{2,3},{5,4},{4,5},{7,6},{6,7},{9,8},{8,9},{11,10... | collective-permute-start | bytes 196616 | tf_op jit(solution)/shard_map/ppermute | solution.py:27

commit v3 on v2

--- a/solution.py
+++ b/solution.py
@@ -26,6 +26,14 @@
         pairs = [(peer(i, distance, count), i) for i in range(count)]
         blocks.append(lax.ppermute(block, axis, pairs))
     return blocks
+
+
+def hop_pairs(count, step):
+    sender = count - step
+    rest = [i for i in range(count) if i not in (sender, sender - 1)]
+    couples = [(sender, sender - 1)] + list(zip(rest[0::2], rest[1::2]))
+    pairs = [pair for a, b in couples for pair in ((a, b), (b, a))]
+    return pairs + [(i, i) for i in rest[len(rest) // 2 * 2 :]]
 
 
 def shifted(plane, row_off, col_off, height, width):
@@ -361,10 +369,9 @@
 
     results = [result]
     received = []
-    ring = [((i + 1) % section_count, i) for i in range(section_count)]
     parcels = None
     for step in range(1, section_count):
-        received.append(lax.ppermute(results[-1], "section", ring))
+        received.append(lax.ppermute(results[-1], "section", hop_pairs(section_count, step)))
         if parcels is None:
             sent = pl.pallas_call(
                 pack_kernel,

time: 40.7 us -> 39.2 us (0.963)
  starting transfers between devices: 21.7 us -> 18.2 us
  waiting for transfers between devices: 9.89 us -> 11.9 us
    ppermute x3, waiting for transfers between devices: 3.16 us -> 6.6 us  [shards(): lax.ppermute(results[-1], 'section', hop_pairs(section_count, step))]
    ppermute x3, starting transfers between devices: 13.5 us -> 10.2 us  [shards(): lax.ppermute(results[-1], 'section', hop_pairs(section_count, step))]
    ppermute x3, waiting for transfers between devices: 2.37 us -> 0.77 us  [shards(): lax.ppermute(sent[distance], 'dp', [(peer(i, distance, crop_count), i) fo...]
  transfers between devices with their start and end apart: 12 -> 12, of which waited for: 9 -> 8; matrix products, arithmetic and copies ran while one was open for 0% -> 0% of each run, Pallas kernels for 14% -> 14%
where the time goes in v3:
time: 39.2 us; the launch traced here: 39.1 us
  starting transfers between devices  18.2 us (46%)
  waiting for transfers between devices  11.9 us (30%)
  Pallas kernels  8.21 us (21%)
  between operations  0.71 us (2%)
    ppermute x3, starting transfers between devices, shards(): lax.ppermute(results[-1], 'section', hop_pairs(section_count, step))  10.2 us
    ppermute x3, waiting for transfers between devices, shards(): lax.ppermute(results[-1], 'section', hop_pairs(section_count, step))  6.6 us
    ppermute x6, starting transfers between devices, neighbours(): blocks.append(lax.ppermute(block, axis, pairs))  6.08 us
    ppermute x6, waiting for transfers between devices, neighbours(): blocks.append(lax.ppermute(block, axis, pairs))  4.56 us
    pallas_call x1, Pallas kernels, shards(): pl.pallas_call(functools.partial(far_kernel, far, channels, shard, scale_...  2.45 us
    pallas_call x1, Pallas kernels, shards(): pl.pallas_call(prepare_kernel, out_shape=(slab, slab, slab, jax.ShapeDtyp...  2.16 us
    ppermute x3, starting transfers between devices, shards(): lax.ppermute(sent[distance], 'dp', [(peer(i, distance, crop_count), i) fo...  1.93 us
    pallas_call x3, Pallas kernels, shards(): step_call(received[-1], pre_all, conv_weight, proj_weight, earlier)  1.37 us
  transfers between devices with their start and end apart: 12, of which 8 were waited for; matrix products, arithmetic and copies ran while one was open for 0% of the time, Pallas kernels for 14%

profile of v3, /device:TPU:0, one launch (start us, length us, event | category | flops | bytes accessed | tf_op | source)
XLA Modules:
  0.0 39.1 jit_solution(5833371235804322196)
XLA Ops:
  0.6 3.0 %collective-permute-start.1 = (bf16[2,1,64,256]{3,2,1,0:T(8,128)(2,1)}, bf16[2,1,64,256]{3,2,1,0:T(8,128)(2,1)S(1)}, u32[]{:S(2)}, u32[]{:S(2)}) collective-permute-start(bf16[2,1,64,256]{3,2,1,0:T(8,128)(2,1)} %bitcast.17), channel_id=1, source_target_pairs={{1,0},{0,1},{3,2},{2,3},{5,4},{4,5},{7,6},{6,7},{9,8},{8,9},{11,10... | collective-permute-start | bytes 196616 | tf_op jit(solution)/shard_map/ppermute | solution.py:27
  3.7 0.1 collective-permute-start
  3.7 2.2 %prepare.1 = (bf16[1,256,128]{2,1,0:T(8,128)(2,1)S(1)}, bf16[1,256,128]{2,1,0:T(8,128)(2,1)S(1)}, bf16[1,256,128]{2,1,0:T(8,128)(2,1)S(1)}, bf16[27,256,256]{2,1,0:T(8,128)(2,1)S(1)}, bf16[256,256]{1,0:T(8,128)(2,1)S(1)}) custom-call(bf16[2,1,64,256]{3,2,1,0:T(8,128)(2,1)} %bitcast.20, bf16[2,1,64,256]{3,2,1,0:T(8,128)(2,1)} %bitcast.18, ...), custom_call_target="tpu_custom_call" | custom-call | tf_op jit(solution)/shard_map/prepare/pallas_call | solution.py:345
  5.9 0.4 collective-permute-done.1.refs_3_
  6.3 1.9 %collective-permute-done.refs_1_ = bf16[2,1,64,256]{3,2,1,0:T(8,128)(2,1)S(1)} collective-permute-done((bf16[2,1,64,256]{3,2,1,0:T(8,128)(2,1)}, bf16[2,1,64,256]{3,2,1,0:T(8,128)(2,1)S(1)}, u32[]{:S(2)}, u32[]{:S(2)}) %collective-permute-start) | collective-permute-done | bytes 65568 | tf_op jit(solution)/shard_map/ppermute | solution.py:27
  8.1 0.1 first_block.1
  8.2 1.6 %collective-permute-start.2 = (bf16[2,256,128]{2,1,0:T(8,128)(2,1)S(1)}, bf16[2,256,128]{2,1,0:T(8,128)(2,1)S(1)}, u32[]{:S(2)}, u32[]{:S(2)}) collective-permute-start(bf16[2,256,128]{2,1,0:T(8,128)(2,1)S(1)} %get-tuple-element.25.refs_0_), channel_id=1, source_target_pairs={{24,16},{16,24},{0,8},{8,0},{25,17},{17,25},{1,9},{9,1},{26,18},{1... | collective-permute-start | bytes 393224 | tf_op jit(solution)/shard_map/ppermute | solution.py:374
  9.9 0.1 pack.1
  10.0 0.1 collective-permute-start.4
  10.1 1.6 %collective-permute-start.5 = (bf16[576,128]{1,0:T(8,128)(2,1)S(1)}, bf16[576,128]{1,0:T(8,128)(2,1)S(1)}, u32[]{:S(2)}, u32[]{:S(2)}) collective-permute-start(bf16[576,128]{1,0:T(8,128)(2,1)S(1)} %get-tuple-element.30), channel_id=1, source_target_pairs={{4,0},{6,2},{0,4},{2,6},{5,1},{7,3},{1,5},{3,7},{12,8},{14,10},{8,... | collective-permute-start | bytes 442376 | tf_op jit(solution)/shard_map/ppermute | solution.py:386
  11.6 0.3 collective-permute-start.6
  11.9 1.4 %collective-permute-done.2.grad_ref.refs_1_ = bf16[2,256,128]{2,1,0:T(8,128)(2,1)S(1)} collective-permute-done((bf16[2,256,128]{2,1,0:T(8,128)(2,1)S(1)}, bf16[2,256,128]{2,1,0:T(8,128)(2,1)S(1)}, u32[]{:S(2)}, u32[]{:S(2)}) %collective-permute-start.2) | collective-permute-done | bytes 131104 | tf_op jit(solution)/shard_map/ppermute | solution.py:374
  13.3 5.0 %collective-permute-start.3 = (bf16[2,256,128]{2,1,0:T(8,128)(2,1)S(1)}, bf16[2,256,128]{2,1,0:T(8,128)(2,1)S(1)}, u32[]{:S(2)}, u32[]{:S(2)}) collective-permute-start(bf16[2,256,128]{2,1,0:T(8,128)(2,1)S(1)} %block.3.refs_1_), channel_id=1, source_target_pairs={{16,8},{8,16},{0,24},{24,0},{17,9},{9,17},{1,25},{25,1},{18,10},{1... | collective-permute-start | bytes 393224 | tf_op jit(solution)/shard_map/ppermute | solution.py:374
  18.3 0.0 collective-permute-done.4.refs_1_.refs_3_
  18.3 0.0 collective-permute-done.5.refs_2_
  18.3 0.8 %collective-permute-done.6.refs_3_ = bf16[576,128]{1,0:T(8,128)(2,1)S(1)} collective-permute-done((bf16[576,128]{1,0:T(8,128)(2,1)S(1)}, bf16[576,128]{1,0:T(8,128)(2,1)S(1)}, u32[]{:S(2)}, u32[]{:S(2)}) %collective-permute-start.6) | collective-permute-done | bytes 147488 | tf_op jit(solution)/shard_map/ppermute | solution.py:386
  19.0 2.3 %collective-permute-done.3.grad_ref.refs_2_ = bf16[2,256,128]{2,1,0:T(8,128)(2,1)S(1)} collective-permute-done((bf16[2,256,128]{2,1,0:T(8,128)(2,1)S(1)}, bf16[2,256,128]{2,1,0:T(8,128)(2,1)S(1)}, u32[]{:S(2)}, u32[]{:S(2)}) %collective-permute-start.3) | collective-permute-done | bytes 131104 | tf_op jit(solution)/shard_map/ppermute | solution.py:374
  21.3 3.6 %collective-permute-start.7 = (bf16[2,256,128]{2,1,0:T(8,128)(2,1)S(1)}, bf16[2,256,128]{2,1,0:T(8,128)(2,1)S(1)}, u32[]{:S(2)}, u32[]{:S(2)}) collective-permute-start(bf16[2,256,128]{2,1,0:T(8,128)(2,1)S(1)} %block.4.refs_2_), channel_id=1, source_target_pairs={{8,0},{0,8},{16,24},{24,16},{9,1},{1,9},{17,25},{25,17},{10,2},{2,... | collective-permute-start | bytes 393224 | tf_op jit(solution)/shard_map/ppermute | solution.py:374
  24.9 3.0 %collective-permute-done.7.grad_ref.refs_3_ = bf16[2,256,128]{2,1,0:T(8,128)(2,1)S(1)} collective-permute-done((bf16[2,256,128]{2,1,0:T(8,128)(2,1)S(1)}, bf16[2,256,128]{2,1,0:T(8,128)(2,1)S(1)}, u32[]{:S(2)}, u32[]{:S(2)}) %collective-permute-start.7) | collective-permute-done | bytes 131104 | tf_op jit(solution)/shard_map/ppermute | solution.py:374
  27.9 0.1 collective-permute-start.11
  28.0 1.6 %collective-permute-start.9 = (bf16[2,256,128]{2,1,0:T(8,128)(2,1)S(1)}, bf16[2,256,128]{2,1,0:T(8,128)(2,1)S(1)}, u32[]{:S(2)}, u32[]{:S(2)}) collective-permute-start(bf16[2,256,128]{2,1,0:T(8,128)(2,1)S(1)} %choose.1.refs_0_), channel_id=1, source_target_pairs={{6,0},{4,2},{2,4},{0,6},{7,1},{5,3},{3,5},{1,7},{14,8},{12,10},{10... | collective-permute-start | bytes 393224 | tf_op jit(solution)/shard_map/ppermute | solution.py:27
  29.6 0.5 %collective-permute-start.8 = (bf16[2,256,128]{2,1,0:T(8,128)(2,1)S(1)}, bf16[2,256,128]{2,1,0:T(8,128)(2,1)S(1)}, u32[]{:S(2)}, u32[]{:S(2)}) collective-permute-start(bf16[2,256,128]{2,1,0:T(8,128)(2,1)S(1)} %choose.1.refs_0_), channel_id=1, source_target_pairs={{4,0},{6,2},{0,4},{2,6},{5,1},{7,3},{1,5},{3,7},{12,8},{14,10},{8,... | collective-permute-start | bytes 393224 | tf_op jit(solution)/shard_map/ppermute | solution.py:27
  30.1 0.8 %collective-permute-start.10 = (bf16[1,256,128]{2,1,0:T(8,128)(2,1)S(1)}, bf16[1,256,128]{2,1,0:T(8,128)(2,1)S(1)}, u32[]{:S(2)}, u32[]{:S(2)}) collective-permute-start(bf16[1,256,128]{2,1,0:T(8,128)(2,1)S(1)} %collect.1.refs_0_), channel_id=1, source_target_pairs={{1,0},{0,1},{3,2},{2,3},{5,4},{4,5},{7,6},{6,7},{9,8},{8,9},{11,10... | collective-permute-start | bytes 196616 | tf_op jit(solution)/shard_map/ppermute | solution.py:27
  30.9 1.4 %block.5.refs_3_.refs_2_ = bf16[2,256,128]{2,1,0:T(8,128)(2,1)S(1)} custom-call(bf16[2,256,128]{2,1,0:T(8,128)(2,1)S(1)} %collective-permute-done.7.grad_ref.refs_3_, bf16[2,256,128]{2,1,0:T(8,128)(2,1)S(1)} %get-tuple-element.26.pre_ref, bf16[27,256,256]{2,1,0:T(8,128)(2,1)S(1)} %get-tuple-element.23.refs_4_.conv_ref, ...), custom_call_target="tpu_custom_call" | custom-call | tf_op jit(solution)/shard_map/block/pallas_call | solution.py:410
  32.2 0.8 %own_grads.1 = bf16[2,1,64,256]{3,2,1,0:T(8,128)(2,1)} custom-call(bf16[2,256,128]{2,1,0:T(8,128)(2,1)S(1)} %get-tuple-element.25.refs_0_, bf16[2,256,128]{2,1,0:T(8,128)(2,1)S(1)} %block.3.refs_1_, bf16[2,256,128]{2,1,0:T(8,128)(2,1)S(1)} %block.4.refs_2_, bf16[2,256,128]{2,1,0:T(8,128)(2,1)S(1)} %block.5.refs_3_.refs_2_), custom_call_target="tpu_custom_call" | custom-call | tf_op jit(solution)/shard_map/own_grads/pallas_call | solution.py:464
  33.0 1.4 %collective-permute-done.10.refs_1_ = bf16[1,256,128]{2,1,0:T(8,128)(2,1)S(1)} collective-permute-done((bf16[1,256,128]{2,1,0:T(8,128)(2,1)S(1)}, bf16[1,256,128]{2,1,0:T(8,128)(2,1)S(1)}, u32[]{:S(2)}, u32[]{:S(2)}) %collective-permute-start.10) | collective-permute-done | bytes 65568 | tf_op jit(solution)/shard_map/ppermute | solution.py:27
  34.4 0.4 %unfold.1 = (bf16[1728,512]{1,0:T(8,128)(2,1)S(1)}, bf16[1728,512]{1,0:T(8,128)(2,1)S(1)}) custom-call(bf16[1,256,128]{2,1,0:T(8,128)(2,1)S(1)} %collect.1.refs_0_, bf16[1,256,128]{2,1,0:T(8,128)(2,1)S(1)} %collective-permute-done.10.refs_1_, bf16[2,256,128]{2,1,0:T(8,128)(2,1)S(1)} %block.5.refs_3_.refs_2_), custom_call_target="tpu_custom_call" | custom-call | tf_op jit(solution)/shard_map/unfold/pallas_call | solution.py:423
  34.8 0.0 collective-permute-done.11.refs_1_
  34.8 0.9 %near_weight_grads.1 = (f32[1728,256]{1,0:T(8,128)S(1)}, f32[64,256]{1,0:T(8,128)S(1)}) custom-call(bf16[2,256,128]{2,1,0:T(8,128)(2,1)S(1)} %choose.1.refs_0_, bf16[2,256,128]{2,1,0:T(8,128)(2,1)S(1)} %collective-permute-done.11.refs_1_, bf16[576,128]{1,0:T(8,128)(2,1)S(1)} %get-tuple-element.28.refs_0_.refs_2_, ...), custom_call_target="tpu_custom_call" | custom-call | tf_op jit(solution)/shard_map/near_weight_grads/pallas_call | solution.py:438
  35.7 0.0 collective-permute-done.9.refs_1_
  35.7 1.0 %collective-permute-done.8.refs_0_ = bf16[2,256,128]{2,1,0:T(8,128)(2,1)S(1)} collective-permute-done((bf16[2,256,128]{2,1,0:T(8,128)(2,1)S(1)}, bf16[2,256,128]{2,1,0:T(8,128)(2,1)S(1)}, u32[]{:S(2)}, u32[]{:S(2)}) %collective-permute-start.8) | collective-permute-done | bytes 131104 | tf_op jit(solution)/shard_map/ppermute | solution.py:27
  36.6 2.4 %far_weight_grads.1 = (f32[1728,256]{1,0:T(8,128)}, f32[64,256]{1,0:T(8,128)}) custom-call(bf16[2,256,128]{2,1,0:T(8,128)(2,1)S(1)} %collective-permute-done.8.refs_0_, bf16[2,256,128]{2,1,0:T(8,128)(2,1)S(1)} %collective-permute-done.9.refs_1_, bf16[576,128]{1,0:T(8,128)(2,1)S(1)} %collective-permute-done.5.refs_2_, ...), custom_call_target="tpu_custom_call" | custom-call | tf_op jit(solution)/shard_map/far_weight_grads/pallas_call | solution.py:450
  (4 shorter events, 0.0 us)
Async XLA Ops:
  0.6 5.6 %collective-permute-start.1 = (bf16[2,1,64,256]{3,2,1,0:T(8,128)(2,1)}, bf16[2,1,64,256]{3,2,1,0:T(8,128)(2,1)S(1)}, u32[]{:S(2)}, u32[]{:S(2)}) collective-permute-start(bf16[2,1,64,256]{3,2,1,0:T(8,128)(2,1)} %bitcast.17), channel_id=1, source_target_pairs={{1,0},{0,1},{3,2},{2,3},{5,4},{4,5},{7,6},{6,7},{9,8},{8,9},{11,10... | collective-permute-start | bytes 196616 | tf_op jit(solution)/shard_map/ppermute | solution.py:27
  3.7 4.5 %collective-permute-start = (bf16[2,1,64,256]{3,2,1,0:T(8,128)(2,1)}, bf16[2,1,64,256]{3,2,1,0:T(8,128)(2,1)S(1)}, u32[]{:S(2)}, u32[]{:S(2)}) collective-permute-start(bf16[2,1,64,256]{3,2,1,0:T(8,128)(2,1)} %bitcast.19), channel_id=1, source_target_pairs={{1,0},{0,1},{3,2},{2,3},{5,4},{4,5},{7,6},{6,7},{9,8},{8,9},{11,10... | collective-permute-start | bytes 196616 | tf_op jit(solution)/shard_map/ppermute | solution.py:27
  8.2 5.0 %collective-permute-start.2 = (bf16[2,256,128]{2,1,0:T(8,128)(2,1)S(1)}, bf16[2,256,128]{2,1,0:T(8,128)(2,1)S(1)}, u32[]{:S(2)}, u32[]{:S(2)}) collective-permute-start(bf16[2,256,128]{2,1,0:T(8,128)(2,1)S(1)} %get-tuple-element.25.refs_0_), channel_id=1, source_target_pairs={{24,16},{16,24},{0,8},{8,0},{25,17},{17,25},{1,9},{9,1},{26,18},{1... | collective-permute-start | bytes 393224 | tf_op jit(solution)/shard_map/ppermute | solution.py:374
  10.0 8.3 %collective-permute-start.4 = (bf16[576,128]{1,0:T(8,128)(2,1)S(1)}, bf16[576,128]{1,0:T(8,128)(2,1)S(1)}, u32[]{:S(2)}, u32[]{:S(2)}) collective-permute-start(bf16[576,128]{1,0:T(8,128)(2,1)S(1)} %get-tuple-element.29), channel_id=1, source_target_pairs={{2,0},{0,2},{6,4},{4,6},{3,1},{1,3},{7,5},{5,7},{10,8},{8,10},{14,... | collective-permute-start | bytes 442376 | tf_op jit(solution)/shard_map/ppermute | solution.py:386
  10.1 8.2 %collective-permute-start.5 = (bf16[576,128]{1,0:T(8,128)(2,1)S(1)}, bf16[576,128]{1,0:T(8,128)(2,1)S(1)}, u32[]{:S(2)}, u32[]{:S(2)}) collective-permute-start(bf16[576,128]{1,0:T(8,128)(2,1)S(1)} %get-tuple-element.30), channel_id=1, source_target_pairs={{4,0},{6,2},{0,4},{2,6},{5,1},{7,3},{1,5},{3,7},{12,8},{14,10},{8,... | collective-permute-start | bytes 442376 | tf_op jit(solution)/shard_map/ppermute | solution.py:386
  11.6 7.4 %collective-permute-start.6 = (bf16[576,128]{1,0:T(8,128)(2,1)S(1)}, bf16[576,128]{1,0:T(8,128)(2,1)S(1)}, u32[]{:S(2)}, u32[]{:S(2)}) collective-permute-start(bf16[576,128]{1,0:T(8,128)(2,1)S(1)} %get-tuple-element.31), channel_id=1, source_target_pairs={{6,0},{4,2},{2,4},{0,6},{7,1},{5,3},{3,5},{1,7},{14,8},{12,10},{10... | collective-permute-start | bytes 442376 | tf_op jit(solution)/shard_map/ppermute | solution.py:386
  13.3 8.0 %collective-permute-start.3 = (bf16[2,256,128]{2,1,0:T(8,128)(2,1)S(1)}, bf16[2,256,128]{2,1,0:T(8,128)(2,1)S(1)}, u32[]{:S(2)}, u32[]{:S(2)}) collective-permute-start(bf16[2,256,128]{2,1,0:T(8,128)(2,1)S(1)} %block.3.refs_1_), channel_id=1, source_target_pairs={{16,8},{8,16},{0,24},{24,0},{17,9},{9,17},{1,25},{25,1},{18,10},{1... | collective-permute-start | bytes 393224 | tf_op jit(solution)/shard_map/ppermute | solution.py:374
  21.3 6.6 %collective-permute-start.7 = (bf16[2,256,128]{2,1,0:T(8,128)(2,1)S(1)}, bf16[2,256,128]{2,1,0:T(8,128)(2,1)S(1)}, u32[]{:S(2)}, u32[]{:S(2)}) collective-permute-start(bf16[2,256,128]{2,1,0:T(8,128)(2,1)S(1)} %block.4.refs_2_), channel_id=1, source_target_pairs={{8,0},{0,8},{16,24},{24,16},{9,1},{1,9},{17,25},{25,17},{10,2},{2,... | collective-permute-start | bytes 393224 | tf_op jit(solution)/shard_map/ppermute | solution.py:374
  27.9 6.9 %collective-permute-start.11 = (bf16[2,256,128]{2,1,0:T(8,128)(2,1)S(1)}, bf16[2,256,128]{2,1,0:T(8,128)(2,1)S(1)}, u32[]{:S(2)}, u32[]{:S(2)}) collective-permute-start(bf16[2,256,128]{2,1,0:T(8,128)(2,1)S(1)} %choose.1.refs_0_), channel_id=1, source_target_pairs={{2,0},{0,2},{6,4},{4,6},{3,1},{1,3},{7,5},{5,7},{10,8},{8,10},{14,... | collective-permute-start | bytes 393224 | tf_op jit(solution)/shard_map/ppermute | solution.py:27
  28.0 7.7 %collective-permute-start.9 = (bf16[2,256,128]{2,1,0:T(8,128)(2,1)S(1)}, bf16[2,256,128]{2,1,0:T(8,128)(2,1)S(1)}, u32[]{:S(2)}, u32[]{:S(2)}) collective-permute-start(bf16[2,256,128]{2,1,0:T(8,128)(2,1)S(1)} %choose.1.refs_0_), channel_id=1, source_target_pairs={{6,0},{4,2},{2,4},{0,6},{7,1},{5,3},{3,5},{1,7},{14,8},{12,10},{10... | collective-permute-start | bytes 393224 | tf_op jit(solution)/shard_map/ppermute | solution.py:27
  29.6 7.1 %collective-permute-start.8 = (bf16[2,256,128]{2,1,0:T(8,128)(2,1)S(1)}, bf16[2,256,128]{2,1,0:T(8,128)(2,1)S(1)}, u32[]{:S(2)}, u32[]{:S(2)}) collective-permute-start(bf16[2,256,128]{2,1,0:T(8,128)(2,1)S(1)} %choose.1.refs_0_), channel_id=1, source_target_pairs={{4,0},{6,2},{0,4},{2,6},{5,1},{7,3},{1,5},{3,7},{12,8},{14,10},{8,... | collective-permute-start | bytes 393224 | tf_op jit(solution)/shard_map/ppermute | solution.py:27
  30.1 4.3 %collective-permute-start.10 = (bf16[1,256,128]{2,1,0:T(8,128)(2,1)S(1)}, bf16[1,256,128]{2,1,0:T(8,128)(2,1)S(1)}, u32[]{:S(2)}, u32[]{:S(2)}) collective-permute-start(bf16[1,256,128]{2,1,0:T(8,128)(2,1)S(1)} %collect.1.refs_0_), channel_id=1, source_target_pairs={{1,0},{0,1},{3,2},{2,3},{5,4},{4,5},{7,6},{6,7},{9,8},{8,9},{11,10... | collective-permute-start | bytes 196616 | tf_op jit(solution)/shard_map/ppermute | solution.py:27

commit v4 on v3

--- a/solution.py
+++ b/solution.py
@@ -28,12 +28,26 @@
     return blocks
 
 
+def relayed(block, axis, handed):
+    count = lax.axis_size(axis)
+    near = count // 2
+    if count & (count - 1) or near < 2:
+        return neighbours(block, axis), [list(range(count))]
+
+    def moved(value, distance):
+        return lax.ppermute(value, axis, [(i ^ distance, i) for i in range(count)])
+
+    across = handed(moved(block, near))
+    blocks = [block] + [moved(block, distance) for distance in range(1, near)]
+    blocks += [across] + [moved(across, distance) for distance in range(1, near)]
+    return blocks, [list(range(near)), [near], list(range(near + 1, count))]
+
+
 def hop_pairs(count, step):
     sender = count - step
-    rest = [i for i in range(count) if i not in (sender, sender - 1)]
-    couples = [(sender, sender - 1)] + list(zip(rest[0::2], rest[1::2]))
-    pairs = [pair for a, b in couples for pair in ((a, b), (b, a))]
-    return pairs + [(i, i) for i in rest[len(rest) // 2 * 2 :]]
+    if sender % 2 == 0 or count % 2 == 1:
+        return [((i + 1) % count, i) for i in range(count)]
+    return [(i ^ 1, i) for i in range(count)]
 
 
 def shifted(plane, row_off, col_off, height, width):
@@ -185,8 +199,8 @@
             ]
 
 
-def unfold_kernel(height, width, others, shard, near, *refs):
-    slab_refs, near_ref, far_ref, scratch = refs[: others + 1], *refs[others + 2 :]
+def unfold_kernel(height, width, others, shard, groups, *refs):
+    slab_refs, group_refs, scratch = refs[: others + 1], refs[others + 2 : -1], refs[-1]
     here = lax.axis_index("space")
     count = lax.axis_size("dp")
     depth_dev, rows, lanes = slab_refs[0].shape
@@ -213,12 +227,18 @@
                 taps.extend(moved[z + depth_off] if inside else [blank] * len(PLANE_TAPS))
             columns.append(jnp.concatenate(taps, axis=0).astype(jnp.bfloat16))
         span = lanes * depth_all
-        target, start = (near_ref, place) if place < near else (far_ref, place - near)
+        target, start = [
+            (ref, place - group[0]) for ref, group in zip(group_refs, groups) if place in group
+        ][0]
         target[:, start * span : (start + 1) * span] = jnp.concatenate(columns, axis=1)
 
 
+def pass_kernel(block_ref, *refs):
+    refs[-1][...] = block_ref[...]
+
+
 def choose_kernel(count, *refs):
-    step_refs, grad_ref = refs[:-1], refs[-1]
+    step_refs, grad_ref = refs[:count], refs[-1]
     section = lax.axis_index("section")
     for step, step_ref in enumerate(step_refs):
 
@@ -256,35 +276,44 @@
     return total
 
 
-def near_kernel(count, channels, shard, *refs):
+def partial_kernel(count, channels, shard, has_before, *refs):
     grad_refs, parcel_refs = refs[:count], refs[count : 2 * count]
-    unfolded_ref, proj_ref, conv_out_ref, proj_out_ref, masked_ref = refs[2 * count :]
-    proj_out_ref[...] = block_terms(
-        grad_refs, parcel_refs, proj_ref, masked_ref, channels, shard
-    )
-    conv_out_ref[...] = lax.dot_general(
+    unfolded_ref, proj_ref, *before_refs, conv_out_ref, proj_out_ref, masked_ref = refs[2 * count :]
+    proj_total = block_terms(grad_refs, parcel_refs, proj_ref, masked_ref, channels, shard)
+    conv_total = lax.dot_general(
         unfolded_ref[...], masked_ref[...], CONTRACT_LANES, preferred_element_type=jnp.float32
     )
-
-
-def far_kernel(count, channels, shard, scale_term, cuts, *refs):
+    if has_before:
+        conv_total = before_refs[0][...] + conv_total
+        proj_total = before_refs[1][...] + proj_total
+    conv_out_ref[...] = conv_total
+    proj_out_ref[...] = proj_total
+
+
+def final_kernel(count, channels, shard, has_before, scale_term, cuts, taps, *refs):
     grad_refs, parcel_refs = refs[:count], refs[count : 2 * count]
-    unfolded_ref, proj_ref, conv_near_ref, proj_near_ref = refs[2 * count : 2 * count + 4]
-    conv_out_ref, proj_out_ref, masked_ref, rows_ref, sems = refs[2 * count + 4 :]
-    proj_far = block_terms(grad_refs, parcel_refs, proj_ref, masked_ref, channels, shard)
-    proj_out_ref[...] = (proj_near_ref[...] + proj_far) * scale_term
-    size = rows_ref.shape[1]
+    unfolded_ref, proj_ref, *before_refs = refs[2 * count : -5]
+    conv_out_ref, proj_out_ref, masked_ref, rows_ref, sems = refs[-5:]
+    proj_total = block_terms(grad_refs, parcel_refs, proj_ref, masked_ref, channels, shard)
+    if has_before:
+        proj_total = before_refs[1][...] + proj_total
+    proj_out_ref[...] = proj_total * scale_term
+    size = taps * shard // cuts
     copies = []
     for cut in range(cuts):
         span = pl.ds(cut * size, size)
-        total = conv_near_ref[span] + lax.dot_general(
+        total = lax.dot_general(
             unfolded_ref[span], masked_ref[...], CONTRACT_LANES, preferred_element_type=jnp.float32
         )
-        rows_ref[cut] = total * scale_term
-        copies.append(
-            pltpu.make_async_copy(rows_ref.at[cut], conv_out_ref.at[span], sems.at[cut])
-        )
-        copies[-1].start()
+        if has_before:
+            total = before_refs[0][span] + total
+        rows_ref[span] = total * scale_term
+        for tap in range(cut * taps // cuts, (cut + 1) * taps // cuts):
+            part = pl.ds(tap * shard, shard)
+            copies.append(
+                pltpu.make_async_copy(rows_ref.at[part], conv_out_ref.at[part], sems.at[tap])
+            )
+            copies[-1].start()
     for copy in copies:
         copy.wait()
 
@@ -416,50 +445,6 @@
         compiler_params=params(),
         name="choose",
     )(grad_first, *received)
-    grad_blocks = neighbours(grad_own, "dp")
-
-    near = crop_count // 2
-    span = planes * lanes
-    near_unfolded, far_unfolded = pl.pallas_call(
-        functools.partial(unfold_kernel, height, width, others, shard, near),
-        out_shape=(
-            jax.ShapeDtypeStruct((taps * shard, near * span), bfloat),
-            jax.ShapeDtypeStruct((taps * shard, (crop_count - near) * span), bfloat),
-        ),
-        in_specs=whole(space_count) + [pl.BlockSpec(memory_space=pl.ANY)],
-        out_specs=tuple(whole(2)),
-        scratch_shapes=[pltpu.VMEM((planes, crop_count * padded, lanes), jnp.float32)],
-        compiler_params=params(),
-        name="unfold",
-    )(*neighbours(acts_mine, "space"), results[-1])
-
-    conv_shape = jax.ShapeDtypeStruct((taps * shard, channels), jnp.float32)
-    proj_shape = jax.ShapeDtypeStruct((shard, channels), jnp.float32)
-    conv_near, proj_near = pl.pallas_call(
-        functools.partial(near_kernel, near, channels, shard),
-        out_shape=(conv_shape, proj_shape),
-        in_specs=whole(2 * near + 2),
-        out_specs=tuple(whole(2)),
-        scratch_shapes=[pltpu.VMEM((channels, near * span), bfloat)],
-        compiler_params=params(),
-        name="near_weight_grads",
-    )(*grad_blocks[:near], *parcels[:near], near_unfolded, proj_weight)
-
-    cuts = len(SIDE) if (len(PLANE_TAPS) * shard) % 16 == 0 else 1
-    far = crop_count - near
-    conv_rows, proj_rows = pl.pallas_call(
-        functools.partial(far_kernel, far, channels, shard, scale_term, cuts),
-        out_shape=(conv_shape, proj_shape),
-        in_specs=whole(2 * far + 4),
-        out_specs=(pl.BlockSpec(memory_space=pltpu.HBM), whole()[0]),
-        scratch_shapes=[
-            pltpu.VMEM((channels, far * span), bfloat),
-            pltpu.VMEM((cuts, taps * shard // cuts, channels), jnp.float32),
-            pltpu.SemaphoreType.DMA((cuts,)),
-        ],
-        compiler_params=params(),
-        name="far_weight_grads",
-    )(*grad_blocks[near:], *parcels[near:], far_unfolded, proj_weight, conv_near, proj_near)
 
     section_out = pl.pallas_call(
         functools.partial(select_kernel, section_count, depth_dev),
@@ -469,6 +454,68 @@
         compiler_params=params(),
         name="own_grads",
     )(*results)
+
+    def handed(value):
+        return pl.pallas_call(
+            pass_kernel,
+            out_shape=volume,
+            in_specs=whole() + [pl.BlockSpec(memory_space=pl.ANY)] * space_count,
+            out_specs=whole()[0],
+            compiler_params=params(),
+            name="hand_on",
+        )(value, *kept_in_hbm(section_out), *slabs[1:])
+
+    slabs = neighbours(acts_mine, "space")
+    grad_blocks, groups = relayed(grad_own, "dp", handed)
+
+    span = planes * lanes
+    unfolded = pl.pallas_call(
+        functools.partial(unfold_kernel, height, width, others, shard, groups),
+        out_shape=tuple(
+            jax.ShapeDtypeStruct((taps * shard, len(group) * span), bfloat) for group in groups
+        ),
+        in_specs=whole(space_count) + [pl.BlockSpec(memory_space=pl.ANY)],
+        out_specs=tuple(whole(len(groups))),
+        scratch_shapes=[pltpu.VMEM((planes, crop_count * padded, lanes), jnp.float32)],
+        compiler_params=params(),
+        name="unfold",
+    )(*slabs, grad_blocks[crop_count // 2])
+
+    conv_shape = jax.ShapeDtypeStruct((taps * shard, channels), jnp.float32)
+    proj_shape = jax.ShapeDtypeStruct((shard, channels), jnp.float32)
+    cuts = len(SIDE) if (len(PLANE_TAPS) * shard) % 16 == 0 else 1
+    sums = ()
+    for group, group_rows in zip(groups, unfolded):
+        size = len(group)
+        operands = [grad_blocks[place] for place in group] + [parcels[place] for place in group]
+        operands += [group_rows, proj_weight, *sums]
+        masked = pltpu.VMEM((channels, size * span), bfloat)
+        if group is not groups[-1]:
+            sums = pl.pallas_call(
+                functools.partial(partial_kernel, size, channels, shard, bool(sums)),
+                out_shape=(conv_shape, proj_shape),
+                in_specs=whole(len(operands)),
+                out_specs=tuple(whole(2)),
+                scratch_shapes=[masked],
+                compiler_params=params(),
+                name="part_weight_grads",
+            )(*operands)
+        else:
+            conv_rows, proj_rows = pl.pallas_call(
+                functools.partial(
+                    final_kernel, size, channels, shard, bool(sums), scale_term, cuts, taps
+                ),
+                out_shape=(conv_shape, proj_shape),
+                in_specs=whole(len(operands)),
+                out_specs=(pl.BlockSpec(memory_space=pltpu.HBM), whole()[0]),
+                scratch_shapes=[
+                    masked,
+                    pltpu.VMEM(conv_shape.shape, jnp.float32),
+                    pltpu.SemaphoreType.DMA((taps,)),
+                ],
+                compiler_params=params(),
+                name="weight_grads",
+            )(*operands)
 
     section_grads = section_out.reshape(inputs.shape)
     grad_conv = conv_rows.reshape(taps, shard, channels).swapaxes(0, 1)[None]

time: 39.2 us -> 36.9 us (0.941)
  waiting for transfers between devices: 11.9 us -> 10.2 us
  starting transfers between devices: 18.2 us -> 16.8 us
  Pallas kernels: 8.21 us -> 8.94 us
    ppermute x6 -> x3, starting transfers between devices: 6.08 us -> 4.08 us  [neighbours(): blocks.append(lax.ppermute(block, axis, pairs))]
    ppermute x0 -> x3, starting transfers between devices: none -> 1.63 us  [moved(): return lax.ppermute(value, axis, [(i ^ distance, i) for i in range(count)])]
    ppermute x6 -> x3, waiting for transfers between devices: 4.56 us -> 3.38 us  [neighbours(): blocks.append(lax.ppermute(block, axis, pairs))]
    ppermute x3, starting transfers between devices: 10.2 us -> 9.14 us  [shards(): lax.ppermute(results[-1], 'section', hop_pairs(section_count, step))]
    pallas_call x2 -> x4, Pallas kernels: 3.32 us -> 4.05 us  [the longest x1 2.56 us: shards(): pl.pallas_call(functools.partial(final_kernel, size, channels, shard, boo...]
    ppermute x3, waiting for transfers between devices: 6.6 us -> 6.06 us  [shards(): lax.ppermute(results[-1], 'section', hop_pairs(section_count, step))]
  transfers between devices with their start and end apart: 12 -> 12, of which waited for: 8 -> 7; matrix products, arithmetic and copies ran while one was open for 0% -> 0% of each run, Pallas kernels for 14% -> 17%
where the time goes in v4:
time: 36.9 us; the launch traced here: 36.7 us
  starting transfers between devices  16.8 us (46%)
  waiting for transfers between devices  10.2 us (28%)
  Pallas kernels  8.94 us (24%)
  between operations  0.72 us (2%)
    ppermute x3, starting transfers between devices, shards(): lax.ppermute(results[-1], 'section', hop_pairs(section_count, step))  9.14 us
    ppermute x3, waiting for transfers between devices, shards(): lax.ppermute(results[-1], 'section', hop_pairs(section_count, step))  6.06 us
    ppermute x3, starting transfers between devices, neighbours(): blocks.append(lax.ppermute(block, axis, pairs))  4.08 us
    ppermute x3, waiting for transfers between devices, neighbours(): blocks.append(lax.ppermute(block, axis, pairs))  3.38 us
    pallas_call x1, Pallas kernels, shards(): pl.pallas_call(functools.partial(final_kernel, size, channels, shard, boo...  2.56 us
    pallas_call x1, Pallas kernels, shards(): pl.pallas_call(prepare_kernel, out_shape=(slab, slab, slab, jax.ShapeDtyp...  2.16 us
    ppermute x3, starting transfers between devices, shards(): lax.ppermute(sent[distance], 'dp', [(peer(i, distance, crop_count), i) fo...  1.93 us
    ppermute x3, starting transfers between devices, moved(): return lax.ppermute(value, axis, [(i ^ distance, i) for i in range(count)])  1.63 us
  transfers between devices with their start and end apart: 12, of which 7 were waited for; matrix products, arithmetic and copies ran while one was open for 0% of the time, Pallas kernels for 17%

profile of v4, /device:TPU:0, one launch (start us, length us, event | category | flops | bytes accessed | tf_op | source)
XLA Modules:
  0.0 36.7 jit_solution(11701606549156126789)
XLA Ops:
  0.6 3.0 %collective-permute-start = (bf16[2,1,64,256]{3,2,1,0:T(8,128)(2,1)}, bf16[2,1,64,256]{3,2,1,0:T(8,128)(2,1)S(1)}, u32[]{:S(2)}, u32[]{:S(2)}) collective-permute-start(bf16[2,1,64,256]{3,2,1,0:T(8,128)(2,1)} %bitcast.18), channel_id=1, source_target_pairs={{1,0},{0,1},{3,2},{2,3},{5,4},{4,5},{7,6},{6,7},{9,8},{8,9},{11,10... | collective-permute-start | bytes 196616 | tf_op jit(solution)/shard_map/ppermute | solution.py:27
  3.7 0.1 collective-permute-start.1
  3.7 2.2 %prepare.1 = (bf16[1,256,128]{2,1,0:T(8,128)(2,1)S(1)}, bf16[1,256,128]{2,1,0:T(8,128)(2,1)S(1)}, bf16[1,256,128]{2,1,0:T(8,128)(2,1)S(1)}, bf16[27,256,256]{2,1,0:T(8,128)(2,1)S(1)}, bf16[256,256]{1,0:T(8,128)(2,1)S(1)}) custom-call(bf16[2,1,64,256]{3,2,1,0:T(8,128)(2,1)} %bitcast.19, bf16[2,1,64,256]{3,2,1,0:T(8,128)(2,1)} %bitcast.21, ...), custom_call_target="tpu_custom_call" | custom-call | tf_op jit(solution)/shard_map/prepare/pallas_call | solution.py:374
  5.9 0.4 collective-permute-done.refs_1_
  6.3 1.9 %collective-permute-done.1.refs_3_ = bf16[2,1,64,256]{3,2,1,0:T(8,128)(2,1)S(1)} collective-permute-done((bf16[2,1,64,256]{3,2,1,0:T(8,128)(2,1)}, bf16[2,1,64,256]{3,2,1,0:T(8,128)(2,1)S(1)}, u32[]{:S(2)}, u32[]{:S(2)}) %collective-permute-start.1) | collective-permute-done | bytes 65568 | tf_op jit(solution)/shard_map/ppermute | solution.py:27
  8.1 0.1 first_block.1
  8.2 1.6 %collective-permute-start.2 = (bf16[2,256,128]{2,1,0:T(8,128)(2,1)S(1)}, bf16[2,256,128]{2,1,0:T(8,128)(2,1)S(1)}, u32[]{:S(2)}, u32[]{:S(2)}) collective-permute-start(bf16[2,256,128]{2,1,0:T(8,128)(2,1)S(1)} %get-tuple-element.28.refs_0_), channel_id=1, source_target_pairs={{8,0},{0,8},{24,16},{16,24},{9,1},{1,9},{25,17},{17,25},{10,2},{2,... | collective-permute-start | bytes 393224 | tf_op jit(solution)/shard_map/ppermute | solution.py:403
  9.9 0.1 pack.1
  10.0 0.1 collective-permute-start.4
  10.1 1.6 %collective-permute-start.5 = (bf16[576,128]{1,0:T(8,128)(2,1)S(1)}, bf16[576,128]{1,0:T(8,128)(2,1)S(1)}, u32[]{:S(2)}, u32[]{:S(2)}) collective-permute-start(bf16[576,128]{1,0:T(8,128)(2,1)S(1)} %get-tuple-element.33), channel_id=1, source_target_pairs={{4,0},{6,2},{0,4},{2,6},{5,1},{7,3},{1,5},{3,7},{12,8},{14,10},{8,... | collective-permute-start | bytes 442376 | tf_op jit(solution)/shard_map/ppermute | solution.py:415
  11.6 0.3 collective-permute-start.6
  11.9 1.4 %collective-permute-done.2.grad_ref.refs_1_ = bf16[2,256,128]{2,1,0:T(8,128)(2,1)S(1)} collective-permute-done((bf16[2,256,128]{2,1,0:T(8,128)(2,1)S(1)}, bf16[2,256,128]{2,1,0:T(8,128)(2,1)S(1)}, u32[]{:S(2)}, u32[]{:S(2)}) %collective-permute-start.2) | collective-permute-done | bytes 131104 | tf_op jit(solution)/shard_map/ppermute | solution.py:403
  13.3 5.0 %collective-permute-start.3 = (bf16[2,256,128]{2,1,0:T(8,128)(2,1)S(1)}, bf16[2,256,128]{2,1,0:T(8,128)(2,1)S(1)}, u32[]{:S(2)}, u32[]{:S(2)}) collective-permute-start(bf16[2,256,128]{2,1,0:T(8,128)(2,1)S(1)} %block.3.refs_1_), channel_id=1, source_target_pairs={{8,0},{16,8},{24,16},{0,24},{9,1},{17,9},{25,17},{1,25},{10,2},{18... | collective-permute-start | bytes 393224 | tf_op jit(solution)/shard_map/ppermute | solution.py:403
  18.3 0.0 collective-permute-done.4.refs_1_.refs_3_
  18.3 0.0 collective-permute-done.5.refs_2_.refs_1_
  18.3 0.8 %collective-permute-done.6.refs_3_.refs_1_ = bf16[576,128]{1,0:T(8,128)(2,1)S(1)} collective-permute-done((bf16[576,128]{1,0:T(8,128)(2,1)S(1)}, bf16[576,128]{1,0:T(8,128)(2,1)S(1)}, u32[]{:S(2)}, u32[]{:S(2)}) %collective-permute-start.6) | collective-permute-done | bytes 147488 | tf_op jit(solution)/shard_map/ppermute | solution.py:415
  19.0 1.7 %collective-permute-done.3.grad_ref.refs_2_ = bf16[2,256,128]{2,1,0:T(8,128)(2,1)S(1)} collective-permute-done((bf16[2,256,128]{2,1,0:T(8,128)(2,1)S(1)}, bf16[2,256,128]{2,1,0:T(8,128)(2,1)S(1)}, u32[]{:S(2)}, u32[]{:S(2)}) %collective-permute-start.3) | collective-permute-done | bytes 131104 | tf_op jit(solution)/shard_map/ppermute | solution.py:403
  20.8 2.5 %collective-permute-start.7 = (bf16[2,256,128]{2,1,0:T(8,128)(2,1)S(1)}, bf16[2,256,128]{2,1,0:T(8,128)(2,1)S(1)}, u32[]{:S(2)}, u32[]{:S(2)}) collective-permute-start(bf16[2,256,128]{2,1,0:T(8,128)(2,1)S(1)} %block.4.refs_2_), channel_id=1, source_target_pairs={{8,0},{0,8},{24,16},{16,24},{9,1},{1,9},{25,17},{17,25},{10,2},{2,... | collective-permute-start | bytes 393224 | tf_op jit(solution)/shard_map/ppermute | solution.py:403
  23.3 2.9 %collective-permute-done.7.grad_ref.refs_3_ = bf16[2,256,128]{2,1,0:T(8,128)(2,1)S(1)} collective-permute-done((bf16[2,256,128]{2,1,0:T(8,128)(2,1)S(1)}, bf16[2,256,128]{2,1,0:T(8,128)(2,1)S(1)}, u32[]{:S(2)}, u32[]{:S(2)}) %collective-permute-start.7) | collective-permute-done | bytes 131104 | tf_op jit(solution)/shard_map/ppermute | solution.py:403
  26.3 1.6 %collective-permute-start.8 = (bf16[2,256,128]{2,1,0:T(8,128)(2,1)S(1)}, bf16[2,256,128]{2,1,0:T(8,128)(2,1)S(1)}, u32[]{:S(2)}, u32[]{:S(2)}) collective-permute-start(bf16[2,256,128]{2,1,0:T(8,128)(2,1)S(1)} %choose.1.refs_0_), channel_id=1, source_target_pairs={{4,0},{6,2},{0,4},{2,6},{5,1},{7,3},{1,5},{3,7},{12,8},{14,10},{8,... | collective-permute-start | bytes 393224 | tf_op jit(solution)/shard_map/ppermute | solution.py:38
  27.8 1.0 %collective-permute-start.9 = (bf16[1,256,128]{2,1,0:T(8,128)(2,1)S(1)}, bf16[1,256,128]{2,1,0:T(8,128)(2,1)S(1)}, u32[]{:S(2)}, u32[]{:S(2)}) collective-permute-start(bf16[1,256,128]{2,1,0:T(8,128)(2,1)S(1)} %collect.1.refs_0_), channel_id=1, source_target_pairs={{1,0},{0,1},{3,2},{2,3},{5,4},{4,5},{7,6},{6,7},{9,8},{8,9},{11,10... | collective-permute-start | bytes 196616 | tf_op jit(solution)/shard_map/ppermute | solution.py:27
  28.8 0.0 collective-permute-start.11
  28.8 1.4 %block.5.refs_3_ = bf16[2,256,128]{2,1,0:T(8,128)(2,1)S(1)} custom-call(bf16[2,256,128]{2,1,0:T(8,128)(2,1)S(1)} %collective-permute-done.7.grad_ref.refs_3_, bf16[2,256,128]{2,1,0:T(8,128)(2,1)S(1)} %get-tuple-element.29.pre_ref, bf16[27,256,256]{2,1,0:T(8,128)(2,1)S(1)} %get-tuple-element.26.refs_4_.conv_ref, ...), custom_call_target="tpu_custom_call" | custom-call | tf_op jit(solution)/shard_map/block/pallas_call | solution.py:439
  30.2 0.8 %own_grads.1.refs_0_ = bf16[2,1,64,256]{3,2,1,0:T(8,128)(2,1)} custom-call(bf16[2,256,128]{2,1,0:T(8,128)(2,1)S(1)} %get-tuple-element.28.refs_0_, bf16[2,256,128]{2,1,0:T(8,128)(2,1)S(1)} %block.3.refs_1_, bf16[2,256,128]{2,1,0:T(8,128)(2,1)S(1)} %block.4.refs_2_, bf16[2,256,128]{2,1,0:T(8,128)(2,1)S(1)} %block.5.refs_3_), custom_call_target="tpu_custom_call" | custom-call | tf_op jit(solution)/shard_map/own_grads/pallas_call | solution.py:449
  30.9 1.2 %collective-permute-done.9.refs_1_ = bf16[1,256,128]{2,1,0:T(8,128)(2,1)S(1)} collective-permute-done((bf16[1,256,128]{2,1,0:T(8,128)(2,1)S(1)}, bf16[1,256,128]{2,1,0:T(8,128)(2,1)S(1)}, u32[]{:S(2)}, u32[]{:S(2)}) %collective-permute-start.9) | collective-permute-done | bytes 65568 | tf_op jit(solution)/shard_map/ppermute | solution.py:27
  32.1 0.0 collective-permute-done.8.block_ref
  32.1 0.1 collective-permute-start.10
  32.2 0.4 %unfold.1 = (bf16[1728,512]{1,0:T(8,128)(2,1)S(1)}, bf16[1728,256]{1,0:T(8,128)(2,1)S(1)}, bf16[1728,256]{1,0:T(8,128)(2,1)S(1)}) custom-call(bf16[1,256,128]{2,1,0:T(8,128)(2,1)S(1)} %collect.1.refs_0_, bf16[1,256,128]{2,1,0:T(8,128)(2,1)S(1)} %collective-permute-done.9.refs_1_, bf16[2,256,128]{2,1,0:T(8,128)(2,1)S(1)} %hand_on.1.refs_2_.refs_0_), custom_call_target="tpu_custom_call" | custom-call | tf_op jit(solution)/shard_map/unfold/pallas_call | solution.py:472
  32.6 0.0 collective-permute-done.11.refs_1_
  32.6 0.9 %part_weight_grads.2 = (f32[1728,256]{1,0:T(8,128)S(1)}, f32[64,256]{1,0:T(8,128)S(1)}) custom-call(bf16[2,256,128]{2,1,0:T(8,128)(2,1)S(1)} %choose.1.refs_0_, bf16[2,256,128]{2,1,0:T(8,128)(2,1)S(1)} %collective-permute-done.11.refs_1_, bf16[576,128]{1,0:T(8,128)(2,1)S(1)} %get-tuple-element.31.refs_0_.refs_2_, ...), custom_call_target="tpu_custom_call" | custom-call | tf_op jit(solution)/shard_map/part_weight_grads/pallas_call | solution.py:494
  33.5 0.6 %part_weight_grads.3 = (f32[1728,256]{1,0:T(8,128)S(1)}, f32[64,256]{1,0:T(8,128)S(1)}) custom-call(bf16[2,256,128]{2,1,0:T(8,128)(2,1)S(1)} %hand_on.1.refs_2_.refs_0_, bf16[576,128]{1,0:T(8,128)(2,1)S(1)} %collective-permute-done.5.refs_2_.refs_1_, bf16[1728,256]{1,0:T(8,128)(2,1)S(1)} %get-tuple-element.37.refs_2_, ...), custom_call_target="tpu_custom_call" | custom-call | tf_op jit(solution)/shard_map/part_weight_grads/pallas_call | solution.py:494
  34.1 0.0 collective-permute-done.10.refs_0_
  34.1 2.6 %weight_grads.1 = (f32[1728,256]{1,0:T(8,128)}, f32[64,256]{1,0:T(8,128)}) custom-call(bf16[2,256,128]{2,1,0:T(8,128)(2,1)S(1)} %collective-permute-done.10.refs_0_, bf16[576,128]{1,0:T(8,128)(2,1)S(1)} %collective-permute-done.6.refs_3_.refs_1_, bf16[1728,256]{1,0:T(8,128)(2,1)S(1)} %get-tuple-element.36.refs_2_, ...), custom_call_target="tpu_custom_call" | custom-call | tf_op jit(solution)/shard_map/weight_grads/pallas_call | solution.py:504
  (5 shorter events, 0.0 us)
Async XLA Ops:
  0.6 5.6 %collective-permute-start = (bf16[2,1,64,256]{3,2,1,0:T(8,128)(2,1)}, bf16[2,1,64,256]{3,2,1,0:T(8,128)(2,1)S(1)}, u32[]{:S(2)}, u32[]{:S(2)}) collective-permute-start(bf16[2,1,64,256]{3,2,1,0:T(8,128)(2,1)} %bitcast.18), channel_id=1, source_target_pairs={{1,0},{0,1},{3,2},{2,3},{5,4},{4,5},{7,6},{6,7},{9,8},{8,9},{11,10... | collective-permute-start | bytes 196616 | tf_op jit(solution)/shard_map/ppermute | solution.py:27
  3.7 4.5 %collective-permute-start.1 = (bf16[2,1,64,256]{3,2,1,0:T(8,128)(2,1)}, bf16[2,1,64,256]{3,2,1,0:T(8,128)(2,1)S(1)}, u32[]{:S(2)}, u32[]{:S(2)}) collective-permute-start(bf16[2,1,64,256]{3,2,1,0:T(8,128)(2,1)} %bitcast.20), channel_id=1, source_target_pairs={{1,0},{0,1},{3,2},{2,3},{5,4},{4,5},{7,6},{6,7},{9,8},{8,9},{11,10... | collective-permute-start | bytes 196616 | tf_op jit(solution)/shard_map/ppermute | solution.py:27
  8.2 5.0 %collective-permute-start.2 = (bf16[2,256,128]{2,1,0:T(8,128)(2,1)S(1)}, bf16[2,256,128]{2,1,0:T(8,128)(2,1)S(1)}, u32[]{:S(2)}, u32[]{:S(2)}) collective-permute-start(bf16[2,256,128]{2,1,0:T(8,128)(2,1)S(1)} %get-tuple-element.28.refs_0_), channel_id=1, source_target_pairs={{8,0},{0,8},{24,16},{16,24},{9,1},{1,9},{25,17},{17,25},{10,2},{2,... | collective-permute-start | bytes 393224 | tf_op jit(solution)/shard_map/ppermute | solution.py:403
  10.0 8.3 %collective-permute-start.4 = (bf16[576,128]{1,0:T(8,128)(2,1)S(1)}, bf16[576,128]{1,0:T(8,128)(2,1)S(1)}, u32[]{:S(2)}, u32[]{:S(2)}) collective-permute-start(bf16[576,128]{1,0:T(8,128)(2,1)S(1)} %get-tuple-element.32), channel_id=1, source_target_pairs={{2,0},{0,2},{6,4},{4,6},{3,1},{1,3},{7,5},{5,7},{10,8},{8,10},{14,... | collective-permute-start | bytes 442376 | tf_op jit(solution)/shard_map/ppermute | solution.py:415
  10.1 8.2 %collective-permute-start.5 = (bf16[576,128]{1,0:T(8,128)(2,1)S(1)}, bf16[576,128]{1,0:T(8,128)(2,1)S(1)}, u32[]{:S(2)}, u32[]{:S(2)}) collective-permute-start(bf16[576,128]{1,0:T(8,128)(2,1)S(1)} %get-tuple-element.33), channel_id=1, source_target_pairs={{4,0},{6,2},{0,4},{2,6},{5,1},{7,3},{1,5},{3,7},{12,8},{14,10},{8,... | collective-permute-start | bytes 442376 | tf_op jit(solution)/shard_map/ppermute | solution.py:415
  11.6 7.4 %collective-permute-start.6 = (bf16[576,128]{1,0:T(8,128)(2,1)S(1)}, bf16[576,128]{1,0:T(8,128)(2,1)S(1)}, u32[]{:S(2)}, u32[]{:S(2)}) collective-permute-start(bf16[576,128]{1,0:T(8,128)(2,1)S(1)} %get-tuple-element.34), channel_id=1, source_target_pairs={{6,0},{4,2},{2,4},{0,6},{7,1},{5,3},{3,5},{1,7},{14,8},{12,10},{10... | collective-permute-start | bytes 442376 | tf_op jit(solution)/shard_map/ppermute | solution.py:415
  13.3 7.5 %collective-permute-start.3 = (bf16[2,256,128]{2,1,0:T(8,128)(2,1)S(1)}, bf16[2,256,128]{2,1,0:T(8,128)(2,1)S(1)}, u32[]{:S(2)}, u32[]{:S(2)}) collective-permute-start(bf16[2,256,128]{2,1,0:T(8,128)(2,1)S(1)} %block.3.refs_1_), channel_id=1, source_target_pairs={{8,0},{16,8},{24,16},{0,24},{9,1},{17,9},{25,17},{1,25},{10,2},{18... | collective-permute-start | bytes 393224 | tf_op jit(solution)/shard_map/ppermute | solution.py:403
  20.8 5.5 %collective-permute-start.7 = (bf16[2,256,128]{2,1,0:T(8,128)(2,1)S(1)}, bf16[2,256,128]{2,1,0:T(8,128)(2,1)S(1)}, u32[]{:S(2)}, u32[]{:S(2)}) collective-permute-start(bf16[2,256,128]{2,1,0:T(8,128)(2,1)S(1)} %block.4.refs_2_), channel_id=1, source_target_pairs={{8,0},{0,8},{24,16},{16,24},{9,1},{1,9},{25,17},{17,25},{10,2},{2,... | collective-permute-start | bytes 393224 | tf_op jit(solution)/shard_map/ppermute | solution.py:403
  26.3 5.8 %collective-permute-start.8 = (bf16[2,256,128]{2,1,0:T(8,128)(2,1)S(1)}, bf16[2,256,128]{2,1,0:T(8,128)(2,1)S(1)}, u32[]{:S(2)}, u32[]{:S(2)}) collective-permute-start(bf16[2,256,128]{2,1,0:T(8,128)(2,1)S(1)} %choose.1.refs_0_), channel_id=1, source_target_pairs={{4,0},{6,2},{0,4},{2,6},{5,1},{7,3},{1,5},{3,7},{12,8},{14,10},{8,... | collective-permute-start | bytes 393224 | tf_op jit(solution)/shard_map/ppermute | solution.py:38
  27.8 4.3 %collective-permute-start.9 = (bf16[1,256,128]{2,1,0:T(8,128)(2,1)S(1)}, bf16[1,256,128]{2,1,0:T(8,128)(2,1)S(1)}, u32[]{:S(2)}, u32[]{:S(2)}) collective-permute-start(bf16[1,256,128]{2,1,0:T(8,128)(2,1)S(1)} %collect.1.refs_0_), channel_id=1, source_target_pairs={{1,0},{0,1},{3,2},{2,3},{5,4},{4,5},{7,6},{6,7},{9,8},{8,9},{11,10... | collective-permute-start | bytes 196616 | tf_op jit(solution)/shard_map/ppermute | solution.py:27
  28.8 3.8 %collective-permute-start.11 = (bf16[2,256,128]{2,1,0:T(8,128)(2,1)S(1)}, bf16[2,256,128]{2,1,0:T(8,128)(2,1)S(1)}, u32[]{:S(2)}, u32[]{:S(2)}) collective-permute-start(bf16[2,256,128]{2,1,0:T(8,128)(2,1)S(1)} %choose.1.refs_0_), channel_id=1, source_target_pairs={{2,0},{0,2},{6,4},{4,6},{3,1},{1,3},{7,5},{5,7},{10,8},{8,10},{14,... | collective-permute-start | bytes 393224 | tf_op jit(solution)/shard_map/ppermute | solution.py:38
  32.1 2.0 %collective-permute-start.10 = (bf16[2,256,128]{2,1,0:T(8,128)(2,1)S(1)}, bf16[2,256,128]{2,1,0:T(8,128)(2,1)S(1)}, u32[]{:S(2)}, u32[]{:S(2)}) collective-permute-start(bf16[2,256,128]{2,1,0:T(8,128)(2,1)S(1)} %hand_on.1.refs_2_.refs_0_), channel_id=1, source_target_pairs={{2,0},{0,2},{6,4},{4,6},{3,1},{1,3},{7,5},{5,7},{10,8},{8,10},{14,... | collective-permute-start | bytes 393224 | tf_op jit(solution)/shard_map/ppermute | solution.py:38

commit v5 on v4

--- a/solution.py
+++ b/solution.py
@@ -40,7 +40,7 @@
     across = handed(moved(block, near))
     blocks = [block] + [moved(block, distance) for distance in range(1, near)]
     blocks += [across] + [moved(across, distance) for distance in range(1, near)]
-    return blocks, [list(range(near)), [near], list(range(near + 1, count))]
+    return blocks, [list(range(near)), list(range(near, count))]
 
 
 def hop_pairs(count, step):
@@ -70,30 +70,35 @@
     lanes = grad[0].shape[1]
     total = joined.astype(jnp.float32)
     parts = [total[:, z * lanes : (z + 1) * lanes] for z in range(planes)]
-    total = jnp.concatenate(parts, axis=1)
     taps = len(PLANE_TAPS)
-    for tap, (row_off, col_off) in enumerate(PLANE_TAPS):
-        moved = jnp.concatenate(
-            [
-                shifted(
-                    masked[:, z * lanes : (z + 1) * lanes], -row_off, -col_off, height, width
-                ).astype(jnp.bfloat16)
-                for z in range(planes)
-            ],
-            axis=1,
-        )
-        blank = jnp.zeros((moved.shape[0], lanes), jnp.bfloat16)
-        for depth, depth_off in enumerate(SIDE):
-            if depth_off == 0:
-                source = moved
-            elif depth_off > 0:
-                source = jnp.concatenate([blank, moved[:, : (planes - 1) * lanes]], axis=1)
-            else:
-                source = jnp.concatenate([moved[:, lanes:], blank], axis=1)
-            total = total + jnp.dot(
-                conv_ref[depth * taps + tap], source, preferred_element_type=jnp.float32
+    moved = jnp.concatenate(
+        [
+            jnp.concatenate(
+                [
+                    shifted(
+                        masked[:, z * lanes : (z + 1) * lanes], -row_off, -col_off, height, width
+                    ).astype(jnp.bfloat16)
+                    for z in range(planes)
+                ],
+                axis=1,
             )
-    return [total[:, z * lanes : (z + 1) * lanes].astype(jnp.bfloat16) for z in range(planes)]
+            for row_off, col_off in PLANE_TAPS
+        ],
+        axis=0,
+    )
+    for depth, depth_off in enumerate(SIDE):
+        weights = jnp.concatenate(
+            [conv_ref[depth * taps + tap] for tap in range(taps)], axis=1
+        )
+        first, last = max(0, -depth_off), planes - max(0, depth_off)
+        if first >= last:
+            continue
+        term = jnp.dot(
+            weights, moved[:, first * lanes : last * lanes], preferred_element_type=jnp.float32
+        )
+        for place, z in enumerate(range(first, last)):
+            parts[z + depth_off] += term[:, place * lanes : (place + 1) * lanes]
+    return [part.astype(jnp.bfloat16) for part in parts]
 
 
 def flipped(rows):
@@ -308,12 +313,10 @@
         if has_before:
             total = before_refs[0][span] + total
         rows_ref[span] = total * scale_term
-        for tap in range(cut * taps // cuts, (cut + 1) * taps // cuts):
-            part = pl.ds(tap * shard, shard)
-            copies.append(
-                pltpu.make_async_copy(rows_ref.at[part], conv_out_ref.at[part], sems.at[tap])
-            )
-            copies[-1].start()
+        copies.append(
+            pltpu.make_async_copy(rows_ref.at[span], conv_out_ref.at[span], sems.at[cut])
+        )
+        copies[-1].start()
     for copy in copies:
         copy.wait()
 
@@ -511,7 +514,7 @@
                 scratch_shapes=[
                     masked,
                     pltpu.VMEM(conv_shape.shape, jnp.float32),
-                    pltpu.SemaphoreType.DMA((taps,)),
+                    pltpu.SemaphoreType.DMA((cuts,)),
                 ],
                 compiler_params=params(),
                 name="weight_grads",

time: 36.9 us -> 36.2 us (0.981)
  Pallas kernels: 8.94 us -> 8.24 us
    pallas_call x2 -> x1, Pallas kernels: 1.47 us -> 0.88 us  [shards(): pl.pallas_call(functools.partial(partial_kernel, size, channels, shard, b...]
  transfers between devices with their start and end apart: 12 -> 12, of which waited for: 7 -> 7; matrix products, arithmetic and copies ran while one was open for 0% -> 0% of each run, Pallas kernels for 17% -> 16%
where the time goes in v5:
time: 36.2 us; the launch traced here: 36 us
  starting transfers between devices  16.8 us (46%)
  waiting for transfers between devices  10.2 us (28%)
  Pallas kernels  8.24 us (23%)
  between operations  0.71 us (2%)
    ppermute x3, starting transfers between devices, shards(): lax.ppermute(results[-1], 'section', hop_pairs(section_count, step))  9.21 us
    ppermute x3, waiting for transfers between devices, shards(): lax.ppermute(results[-1], 'section', hop_pairs(section_count, step))  6.08 us
    ppermute x3, starting transfers between devices, neighbours(): blocks.append(lax.ppermute(block, axis, pairs))  4.08 us
    ppermute x3, waiting for transfers between devices, neighbours(): blocks.append(lax.ppermute(block, axis, pairs))  3.37 us
    pallas_call x1, Pallas kernels, shards(): pl.pallas_call(functools.partial(final_kernel, size, channels, shard, boo...  2.45 us
    pallas_call x1, Pallas kernels, shards(): pl.pallas_call(prepare_kernel, out_shape=(slab, slab, slab, jax.ShapeDtyp...  2.16 us
    ppermute x3, starting transfers between devices, shards(): lax.ppermute(sent[distance], 'dp', [(peer(i, distance, crop_count), i) fo...  1.93 us
    ppermute x3, starting transfers between devices, moved(): return lax.ppermute(value, axis, [(i ^ distance, i) for i in range(count)])  1.63 us
  transfers between devices with their start and end apart: 12, of which 7 were waited for; matrix products, arithmetic and copies ran while one was open for 0% of the time, Pallas kernels for 16%

profile of v5, /device:TPU:0, one launch (start us, length us, event | category | flops | bytes accessed | tf_op | source)
XLA Modules:
  0.0 36.0 jit_solution(7078351685866724308)
XLA Ops:
  0.6 3.0 %collective-permute-start = (bf16[2,1,64,256]{3,2,1,0:T(8,128)(2,1)}, bf16[2,1,64,256]{3,2,1,0:T(8,128)(2,1)S(1)}, u32[]{:S(2)}, u32[]{:S(2)}) collective-permute-start(bf16[2,1,64,256]{3,2,1,0:T(8,128)(2,1)} %bitcast.18), channel_id=1, source_target_pairs={{1,0},{0,1},{3,2},{2,3},{5,4},{4,5},{7,6},{6,7},{9,8},{8,9},{11,10... | collective-permute-start | bytes 196616 | tf_op jit(solution)/shard_map/ppermute | solution.py:27
  3.7 0.1 collective-permute-start.1
  3.7 2.2 %prepare.1 = (bf16[1,256,128]{2,1,0:T(8,128)(2,1)S(1)}, bf16[1,256,128]{2,1,0:T(8,128)(2,1)S(1)}, bf16[1,256,128]{2,1,0:T(8,128)(2,1)S(1)}, bf16[27,256,256]{2,1,0:T(8,128)(2,1)S(1)}, bf16[256,256]{1,0:T(8,128)(2,1)S(1)}) custom-call(bf16[2,1,64,256]{3,2,1,0:T(8,128)(2,1)} %bitcast.19, bf16[2,1,64,256]{3,2,1,0:T(8,128)(2,1)} %bitcast.21, ...), custom_call_target="tpu_custom_call" | custom-call | tf_op jit(solution)/shard_map/prepare/pallas_call | solution.py:377
  5.9 0.4 collective-permute-done.refs_1_
  6.3 1.9 %collective-permute-done.1.refs_3_ = bf16[2,1,64,256]{3,2,1,0:T(8,128)(2,1)S(1)} collective-permute-done((bf16[2,1,64,256]{3,2,1,0:T(8,128)(2,1)}, bf16[2,1,64,256]{3,2,1,0:T(8,128)(2,1)S(1)}, u32[]{:S(2)}, u32[]{:S(2)}) %collective-permute-start.1) | collective-permute-done | bytes 65568 | tf_op jit(solution)/shard_map/ppermute | solution.py:27
  8.1 0.1 first_block.1
  8.2 1.6 %collective-permute-start.2 = (bf16[2,256,128]{2,1,0:T(8,128)(2,1)S(1)}, bf16[2,256,128]{2,1,0:T(8,128)(2,1)S(1)}, u32[]{:S(2)}, u32[]{:S(2)}) collective-permute-start(bf16[2,256,128]{2,1,0:T(8,128)(2,1)S(1)} %get-tuple-element.25.refs_0_), channel_id=1, source_target_pairs={{8,0},{0,8},{24,16},{16,24},{9,1},{1,9},{25,17},{17,25},{10,2},{2,... | collective-permute-start | bytes 393224 | tf_op jit(solution)/shard_map/ppermute | solution.py:406
  9.9 0.1 pack.1
  10.0 0.1 collective-permute-start.4
  10.1 1.6 %collective-permute-start.5 = (bf16[576,128]{1,0:T(8,128)(2,1)S(1)}, bf16[576,128]{1,0:T(8,128)(2,1)S(1)}, u32[]{:S(2)}, u32[]{:S(2)}) collective-permute-start(bf16[576,128]{1,0:T(8,128)(2,1)S(1)} %get-tuple-element.30), channel_id=1, source_target_pairs={{4,0},{6,2},{0,4},{2,6},{5,1},{7,3},{1,5},{3,7},{12,8},{14,10},{8,... | collective-permute-start | bytes 442376 | tf_op jit(solution)/shard_map/ppermute | solution.py:418
  11.6 0.3 collective-permute-start.6
  11.9 1.4 %collective-permute-done.2.grad_ref.refs_1_ = bf16[2,256,128]{2,1,0:T(8,128)(2,1)S(1)} collective-permute-done((bf16[2,256,128]{2,1,0:T(8,128)(2,1)S(1)}, bf16[2,256,128]{2,1,0:T(8,128)(2,1)S(1)}, u32[]{:S(2)}, u32[]{:S(2)}) %collective-permute-start.2) | collective-permute-done | bytes 131104 | tf_op jit(solution)/shard_map/ppermute | solution.py:406
  13.3 5.0 %collective-permute-start.3 = (bf16[2,256,128]{2,1,0:T(8,128)(2,1)S(1)}, bf16[2,256,128]{2,1,0:T(8,128)(2,1)S(1)}, u32[]{:S(2)}, u32[]{:S(2)}) collective-permute-start(bf16[2,256,128]{2,1,0:T(8,128)(2,1)S(1)} %block.3.refs_1_), channel_id=1, source_target_pairs={{8,0},{16,8},{24,16},{0,24},{9,1},{17,9},{25,17},{1,25},{10,2},{18... | collective-permute-start | bytes 393224 | tf_op jit(solution)/shard_map/ppermute | solution.py:406
  18.3 0.0 collective-permute-done.4.refs_1_.refs_3_
  18.3 0.0 collective-permute-done.5.refs_2_
  18.3 0.7 %collective-permute-done.6.refs_3_ = bf16[576,128]{1,0:T(8,128)(2,1)S(1)} collective-permute-done((bf16[576,128]{1,0:T(8,128)(2,1)S(1)}, bf16[576,128]{1,0:T(8,128)(2,1)S(1)}, u32[]{:S(2)}, u32[]{:S(2)}) %collective-permute-start.6) | collective-permute-done | bytes 147488 | tf_op jit(solution)/shard_map/ppermute | solution.py:418
  19.0 1.8 %collective-permute-done.3.grad_ref.refs_2_ = bf16[2,256,128]{2,1,0:T(8,128)(2,1)S(1)} collective-permute-done((bf16[2,256,128]{2,1,0:T(8,128)(2,1)S(1)}, bf16[2,256,128]{2,1,0:T(8,128)(2,1)S(1)}, u32[]{:S(2)}, u32[]{:S(2)}) %collective-permute-start.3) | collective-permute-done | bytes 131104 | tf_op jit(solution)/shard_map/ppermute | solution.py:406
  20.8 2.6 %collective-permute-start.7 = (bf16[2,256,128]{2,1,0:T(8,128)(2,1)S(1)}, bf16[2,256,128]{2,1,0:T(8,128)(2,1)S(1)}, u32[]{:S(2)}, u32[]{:S(2)}) collective-permute-start(bf16[2,256,128]{2,1,0:T(8,128)(2,1)S(1)} %block.4.refs_2_), channel_id=1, source_target_pairs={{8,0},{0,8},{24,16},{16,24},{9,1},{1,9},{25,17},{17,25},{10,2},{2,... | collective-permute-start | bytes 393224 | tf_op jit(solution)/shard_map/ppermute | solution.py:406
  23.4 2.9 %collective-permute-done.7.grad_ref.refs_3_ = bf16[2,256,128]{2,1,0:T(8,128)(2,1)S(1)} collective-permute-done((bf16[2,256,128]{2,1,0:T(8,128)(2,1)S(1)}, bf16[2,256,128]{2,1,0:T(8,128)(2,1)S(1)}, u32[]{:S(2)}, u32[]{:S(2)}) %collective-permute-start.7) | collective-permute-done | bytes 131104 | tf_op jit(solution)/shard_map/ppermute | solution.py:406
  26.3 1.6 %collective-permute-start.8 = (bf16[2,256,128]{2,1,0:T(8,128)(2,1)S(1)}, bf16[2,256,128]{2,1,0:T(8,128)(2,1)S(1)}, u32[]{:S(2)}, u32[]{:S(2)}) collective-permute-start(bf16[2,256,128]{2,1,0:T(8,128)(2,1)S(1)} %choose.1.refs_0_), channel_id=1, source_target_pairs={{4,0},{6,2},{0,4},{2,6},{5,1},{7,3},{1,5},{3,7},{12,8},{14,10},{8,... | collective-permute-start | bytes 393224 | tf_op jit(solution)/shard_map/ppermute | solution.py:38
  27.9 1.0 %collective-permute-start.9 = (bf16[1,256,128]{2,1,0:T(8,128)(2,1)S(1)}, bf16[1,256,128]{2,1,0:T(8,128)(2,1)S(1)}, u32[]{:S(2)}, u32[]{:S(2)}) collective-permute-start(bf16[1,256,128]{2,1,0:T(8,128)(2,1)S(1)} %collect.1.refs_0_), channel_id=1, source_target_pairs={{1,0},{0,1},{3,2},{2,3},{5,4},{4,5},{7,6},{6,7},{9,8},{8,9},{11,10... | collective-permute-start | bytes 196616 | tf_op jit(solution)/shard_map/ppermute | solution.py:27
  28.9 0.0 collective-permute-start.11
  28.9 1.4 %block.5.refs_3_ = bf16[2,256,128]{2,1,0:T(8,128)(2,1)S(1)} custom-call(bf16[2,256,128]{2,1,0:T(8,128)(2,1)S(1)} %collective-permute-done.7.grad_ref.refs_3_, bf16[2,256,128]{2,1,0:T(8,128)(2,1)S(1)} %get-tuple-element.26.pre_ref, bf16[27,256,256]{2,1,0:T(8,128)(2,1)S(1)} %get-tuple-element.23.refs_4_.conv_ref, ...), custom_call_target="tpu_custom_call" | custom-call | tf_op jit(solution)/shard_map/block/pallas_call | solution.py:442
  30.3 0.8 %own_grads.1.refs_0_ = bf16[2,1,64,256]{3,2,1,0:T(8,128)(2,1)} custom-call(bf16[2,256,128]{2,1,0:T(8,128)(2,1)S(1)} %get-tuple-element.25.refs_0_, bf16[2,256,128]{2,1,0:T(8,128)(2,1)S(1)} %block.3.refs_1_, bf16[2,256,128]{2,1,0:T(8,128)(2,1)S(1)} %block.4.refs_2_, bf16[2,256,128]{2,1,0:T(8,128)(2,1)S(1)} %block.5.refs_3_), custom_call_target="tpu_custom_call" | custom-call | tf_op jit(solution)/shard_map/own_grads/pallas_call | solution.py:452
  31.0 1.1 %collective-permute-done.9.refs_1_ = bf16[1,256,128]{2,1,0:T(8,128)(2,1)S(1)} collective-permute-done((bf16[1,256,128]{2,1,0:T(8,128)(2,1)S(1)}, bf16[1,256,128]{2,1,0:T(8,128)(2,1)S(1)}, u32[]{:S(2)}, u32[]{:S(2)}) %collective-permute-start.9) | collective-permute-done | bytes 65568 | tf_op jit(solution)/shard_map/ppermute | solution.py:27
  32.2 0.0 collective-permute-done.8.block_ref
  32.2 0.1 collective-permute-start.10
  32.3 0.4 %unfold.1 = (bf16[1728,512]{1,0:T(8,128)(2,1)S(1)}, bf16[1728,512]{1,0:T(8,128)(2,1)S(1)}) custom-call(bf16[1,256,128]{2,1,0:T(8,128)(2,1)S(1)} %collect.1.refs_0_, bf16[1,256,128]{2,1,0:T(8,128)(2,1)S(1)} %collective-permute-done.9.refs_1_, bf16[2,256,128]{2,1,0:T(8,128)(2,1)S(1)} %hand_on.1.refs_2_.refs_0_), custom_call_target="tpu_custom_call" | custom-call | tf_op jit(solution)/shard_map/unfold/pallas_call | solution.py:475
  32.7 0.0 collective-permute-done.11.refs_1_
  32.7 0.9 %part_weight_grads.1 = (f32[1728,256]{1,0:T(8,128)S(1)}, f32[64,256]{1,0:T(8,128)S(1)}) custom-call(bf16[2,256,128]{2,1,0:T(8,128)(2,1)S(1)} %choose.1.refs_0_, bf16[2,256,128]{2,1,0:T(8,128)(2,1)S(1)} %collective-permute-done.11.refs_1_, bf16[576,128]{1,0:T(8,128)(2,1)S(1)} %get-tuple-element.28.refs_0_.refs_2_, ...), custom_call_target="tpu_custom_call" | custom-call | tf_op jit(solution)/shard_map/part_weight_grads/pallas_call | solution.py:497
  33.5 0.0 collective-permute-done.10.refs_1_
  33.6 2.4 %weight_grads.1 = (f32[1728,256]{1,0:T(8,128)}, f32[64,256]{1,0:T(8,128)}) custom-call(bf16[2,256,128]{2,1,0:T(8,128)(2,1)S(1)} %hand_on.1.refs_2_.refs_0_, bf16[2,256,128]{2,1,0:T(8,128)(2,1)S(1)} %collective-permute-done.10.refs_1_, bf16[576,128]{1,0:T(8,128)(2,1)S(1)} %collective-permute-done.5.refs_2_, ...), custom_call_target="tpu_custom_call" | custom-call | tf_op jit(solution)/shard_map/weight_grads/pallas_call | solution.py:507
  (5 shorter events, 0.0 us)
Async XLA Ops:
  0.6 5.6 %collective-permute-start = (bf16[2,1,64,256]{3,2,1,0:T(8,128)(2,1)}, bf16[2,1,64,256]{3,2,1,0:T(8,128)(2,1)S(1)}, u32[]{:S(2)}, u32[]{:S(2)}) collective-permute-start(bf16[2,1,64,256]{3,2,1,0:T(8,128)(2,1)} %bitcast.18), channel_id=1, source_target_pairs={{1,0},{0,1},{3,2},{2,3},{5,4},{4,5},{7,6},{6,7},{9,8},{8,9},{11,10... | collective-permute-start | bytes 196616 | tf_op jit(solution)/shard_map/ppermute | solution.py:27
  3.7 4.5 %collective-permute-start.1 = (bf16[2,1,64,256]{3,2,1,0:T(8,128)(2,1)}, bf16[2,1,64,256]{3,2,1,0:T(8,128)(2,1)S(1)}, u32[]{:S(2)}, u32[]{:S(2)}) collective-permute-start(bf16[2,1,64,256]{3,2,1,0:T(8,128)(2,1)} %bitcast.20), channel_id=1, source_target_pairs={{1,0},{0,1},{3,2},{2,3},{5,4},{4,5},{7,6},{6,7},{9,8},{8,9},{11,10... | collective-permute-start | bytes 196616 | tf_op jit(solution)/shard_map/ppermute | solution.py:27
  8.2 5.0 %collective-permute-start.2 = (bf16[2,256,128]{2,1,0:T(8,128)(2,1)S(1)}, bf16[2,256,128]{2,1,0:T(8,128)(2,1)S(1)}, u32[]{:S(2)}, u32[]{:S(2)}) collective-permute-start(bf16[2,256,128]{2,1,0:T(8,128)(2,1)S(1)} %get-tuple-element.25.refs_0_), channel_id=1, source_target_pairs={{8,0},{0,8},{24,16},{16,24},{9,1},{1,9},{25,17},{17,25},{10,2},{2,... | collective-permute-start | bytes 393224 | tf_op jit(solution)/shard_map/ppermute | solution.py:406
  10.0 8.3 %collective-permute-start.4 = (bf16[576,128]{1,0:T(8,128)(2,1)S(1)}, bf16[576,128]{1,0:T(8,128)(2,1)S(1)}, u32[]{:S(2)}, u32[]{:S(2)}) collective-permute-start(bf16[576,128]{1,0:T(8,128)(2,1)S(1)} %get-tuple-element.29), channel_id=1, source_target_pairs={{2,0},{0,2},{6,4},{4,6},{3,1},{1,3},{7,5},{5,7},{10,8},{8,10},{14,... | collective-permute-start | bytes 442376 | tf_op jit(solution)/shard_map/ppermute | solution.py:418
  10.1 8.2 %collective-permute-start.5 = (bf16[576,128]{1,0:T(8,128)(2,1)S(1)}, bf16[576,128]{1,0:T(8,128)(2,1)S(1)}, u32[]{:S(2)}, u32[]{:S(2)}) collective-permute-start(bf16[576,128]{1,0:T(8,128)(2,1)S(1)} %get-tuple-element.30), channel_id=1, source_target_pairs={{4,0},{6,2},{0,4},{2,6},{5,1},{7,3},{1,5},{3,7},{12,8},{14,10},{8,... | collective-permute-start | bytes 442376 | tf_op jit(solution)/shard_map/ppermute | solution.py:418
  11.6 7.4 %collective-permute-start.6 = (bf16[576,128]{1,0:T(8,128)(2,1)S(1)}, bf16[576,128]{1,0:T(8,128)(2,1)S(1)}, u32[]{:S(2)}, u32[]{:S(2)}) collective-permute-start(bf16[576,128]{1,0:T(8,128)(2,1)S(1)} %get-tuple-element.31), channel_id=1, source_target_pairs={{6,0},{4,2},{2,4},{0,6},{7,1},{5,3},{3,5},{1,7},{14,8},{12,10},{10... | collective-permute-start | bytes 442376 | tf_op jit(solution)/shard_map/ppermute | solution.py:418
  13.3 7.5 %collective-permute-start.3 = (bf16[2,256,128]{2,1,0:T(8,128)(2,1)S(1)}, bf16[2,256,128]{2,1,0:T(8,128)(2,1)S(1)}, u32[]{:S(2)}, u32[]{:S(2)}) collective-permute-start(bf16[2,256,128]{2,1,0:T(8,128)(2,1)S(1)} %block.3.refs_1_), channel_id=1, source_target_pairs={{8,0},{16,8},{24,16},{0,24},{9,1},{17,9},{25,17},{1,25},{10,2},{18... | collective-permute-start | bytes 393224 | tf_op jit(solution)/shard_map/ppermute | solution.py:406
  20.8 5.5 %collective-permute-start.7 = (bf16[2,256,128]{2,1,0:T(8,128)(2,1)S(1)}, bf16[2,256,128]{2,1,0:T(8,128)(2,1)S(1)}, u32[]{:S(2)}, u32[]{:S(2)}) collective-permute-start(bf16[2,256,128]{2,1,0:T(8,128)(2,1)S(1)} %block.4.refs_2_), channel_id=1, source_target_pairs={{8,0},{0,8},{24,16},{16,24},{9,1},{1,9},{25,17},{17,25},{10,2},{2,... | collective-permute-start | bytes 393224 | tf_op jit(solution)/shard_map/ppermute | solution.py:406
  26.3 5.8 %collective-permute-start.8 = (bf16[2,256,128]{2,1,0:T(8,128)(2,1)S(1)}, bf16[2,256,128]{2,1,0:T(8,128)(2,1)S(1)}, u32[]{:S(2)}, u32[]{:S(2)}) collective-permute-start(bf16[2,256,128]{2,1,0:T(8,128)(2,1)S(1)} %choose.1.refs_0_), channel_id=1, source_target_pairs={{4,0},{6,2},{0,4},{2,6},{5,1},{7,3},{1,5},{3,7},{12,8},{14,10},{8,... | collective-permute-start | bytes 393224 | tf_op jit(solution)/shard_map/ppermute | solution.py:38
  27.9 4.3 %collective-permute-start.9 = (bf16[1,256,128]{2,1,0:T(8,128)(2,1)S(1)}, bf16[1,256,128]{2,1,0:T(8,128)(2,1)S(1)}, u32[]{:S(2)}, u32[]{:S(2)}) collective-permute-start(bf16[1,256,128]{2,1,0:T(8,128)(2,1)S(1)} %collect.1.refs_0_), channel_id=1, source_target_pairs={{1,0},{0,1},{3,2},{2,3},{5,4},{4,5},{7,6},{6,7},{9,8},{8,9},{11,10... | collective-permute-start | bytes 196616 | tf_op jit(solution)/shard_map/ppermute | solution.py:27
  28.9 3.8 %collective-permute-start.11 = (bf16[2,256,128]{2,1,0:T(8,128)(2,1)S(1)}, bf16[2,256,128]{2,1,0:T(8,128)(2,1)S(1)}, u32[]{:S(2)}, u32[]{:S(2)}) collective-permute-start(bf16[2,256,128]{2,1,0:T(8,128)(2,1)S(1)} %choose.1.refs_0_), channel_id=1, source_target_pairs={{2,0},{0,2},{6,4},{4,6},{3,1},{1,3},{7,5},{5,7},{10,8},{8,10},{14,... | collective-permute-start | bytes 393224 | tf_op jit(solution)/shard_map/ppermute | solution.py:38
  32.2 1.4 %collective-permute-start.10 = (bf16[2,256,128]{2,1,0:T(8,128)(2,1)S(1)}, bf16[2,256,128]{2,1,0:T(8,128)(2,1)S(1)}, u32[]{:S(2)}, u32[]{:S(2)}) collective-permute-start(bf16[2,256,128]{2,1,0:T(8,128)(2,1)S(1)} %hand_on.1.refs_2_.refs_0_), channel_id=1, source_target_pairs={{2,0},{0,2},{6,4},{4,6},{3,1},{1,3},{7,5},{5,7},{10,8},{8,10},{14,... | collective-permute-start | bytes 393224 | tf_op jit(solution)/shard_map/ppermute | solution.py:38
